TPU v7x, 256 devices: a whole 4x4x8 slice. The times are simulated.
256 devices in a mesh: group: 8 (over y, core), dev: 32 (over x, z).
Axes of the slice: x: 4, y: 4, z: 8, core: 2. Of those that a mesh axis runs over, the one named last changes fastest.
Arguments:
- residual: float32 [192, 768, 144], P('group', 'dev'), may hold values from -6 to 6
- fdm_vectors: float32 [3, 8, 8, 98304], P(None, None, None, ('group', 'dev')), may hold values from -2 to 2
- fdm_values: float32 [3, 8, 98304], P(None, None, ('group', 'dev')), may hold values from 0.1 to 10
- corner_slot: int32 [8, 98304], P(None, ('group', 'dev')), may hold values from 0 to 624, as said below
- x_local: float32 [163840, 128], P(('group', 'dev')), may hold values from -0.07848767 to 0.07848767
- x_middle: float32 [163840, 128], P(('group', 'dev')), may hold values from -0.033 to 0.033
- x_top: float32 [163840, 128], P(('group', 'dev')), may hold values from -0.019621918 to 0.019621918
Outputs:
- preconditioned: float32 [192, 768, 144], P('group', 'dev')
Inputs may be any that keep to these rules, and one draw needn't show every extreme that they name: `corner_slot`: within a block the corners of its 384 elements that coincide share one slot and distinct vertices of the block have distinct slots; the 625 vertices of each block take the slots 0 to 624 in an order drawn per block.
All inputs are finite; a program needn't handle non-finite values.
Results may differ from a plain program's by a relative error of at most 0.0001.
Values sent between devices are 32-bit elements; how exact they have to be, the bound alone decides.
A program may use at most 64 MiB of HBM per device.

v0:
```python
import functools

import jax
import jax.numpy as jnp
import ml_dtypes
import numpy as np
from jax import lax
from jax.experimental import pallas as pl
from jax.experimental.pallas import tpu as pltpu
from jax.sharding import PartitionSpec as P

F32 = jnp.float32
BF16 = jnp.bfloat16
MESH = pl.DeviceIdType.MESH

BX, BY, BZ = 4, 4, 24
NX, NY, NZ = 6 * BX, 6 * BY, 6 * BZ
ELEMENTS = BX * BY * BZ
ROWS = 32
PLANES = NX + 2
LANES = 640
COARSE = 640
SIDES = ((1, 0), (-1, 0), (0, 1), (0, -1), (1, 1), (1, -1), (-1, 1), (-1, -1))


def row_of(y):
    return {0: 24, 25: 25}.get(y, y - 1)


def tables():
    bf16 = ml_dtypes.bfloat16
    pick_z = np.zeros((8 * BZ, NZ), np.float32)
    for l in range(BZ):
        for c in range(8):
            z = 6 * l + c - 1
            if 0 <= z < NZ:
                pick_z[8 * l + c, z] = 1
    pick_y = np.zeros((128, 128), np.float32)
    for i in range(4):
        for b in range(8):
            for j in range(4):
                pick_y[i * 32 + row_of(6 * j + b), i * 32 + b * 4 + j] = 1
    order = np.zeros((ELEMENTS, ELEMENTS), np.float32)
    for i in range(BX):
        for j in range(BY):
            for l in range(BZ):
                order[(i * BY + j) * BZ + l, l // 8 * 128 + i * 32 + l % 8 * 4 + j] = 1

    def hats(elements):
        weights = np.zeros((6 * elements, elements + 1), np.float32)
        for e in range(elements):
            for m in range(6):
                weights[6 * e + m, e] = 11 - 2 * m
                weights[6 * e + m, e + 1] = 2 * m + 1
        return weights

    hat_x, hat_y, hat_z = hats(BX), hats(BY), hats(BZ)
    hat_xy = np.zeros((NX, ROWS, 32), np.float32)
    hat_xy[:, :NY, :25] = np.einsum("xv,yw->xyvw", hat_x, hat_y).reshape(NX, NY, 25)
    hat_xy = hat_xy.reshape(NX * ROWS, 32)
    hat_zw = np.zeros((NZ, LANES), np.float32)
    is_xy = np.zeros((32, LANES), np.float32)
    pick_e = np.zeros((ELEMENTS, LANES), np.float32)
    is_corner = np.zeros((8, LANES), np.float32)
    for vx in range(5):
        for vy in range(5):
            for vz in range(25):
                w = (vx * 5 + vy) * 25 + vz
                hat_zw[:, w] = hat_z[:, vz]
                is_xy[vx * 5 + vy, w] = 1
                i, j, l = min(vx, 3), min(vy, 3), min(vz, 23)
                pick_e[(i * BY + j) * BZ + l, w] = 1
                is_corner[4 * (vx - i) + 2 * (vy - j) + (vz - l), w] = 1
    return (
        pick_z.astype(bf16),
        pick_z.T.copy().astype(bf16),
        pick_y.astype(bf16),
        order.astype(bf16),
        hat_xy.astype(bf16),
        hat_xy.T.copy().astype(bf16),
        hat_zw.astype(bf16),
        pick_e.astype(bf16),
        is_xy,
        is_corner,
    )


def split(value):
    high = value.astype(BF16)
    return high, (value - high.astype(F32)).astype(BF16)


def mm(a, b):
    return lax.dot_general(a, b, (((1,), (0,)), ((), ())), preferred_element_type=F32)


def mm_t(a, b):
    return lax.dot_general(a, b, (((1,), (1,)), ((), ())), preferred_element_type=F32)


def swap_chunks(pieces, masks):
    pieces = list(pieces)
    for bit in range(3):
        shift = 4 << bit
        mask = masks[bit]
        for low in range(8):
            if low >> bit & 1:
                continue
            high = low | 1 << bit
            x, y = pieces[low], pieces[high]
            pieces[low] = jnp.where(mask, pltpu.roll(y, shift, 1), x)
            pieces[high] = jnp.where(mask, y, pltpu.roll(x, 128 - shift, 1))
    return pieces


def kernel(
    n_group,
    n_dev,
    residual,
    vectors_in,
    values_in,
    slot_in,
    x_local_in,
    x_middle_in,
    x_top_in,
    pick_z_in,
    pick_zt_in,
    pick_y_in,
    order_in,
    hat_xy_in,
    hat_xyt_in,
    hat_zw_in,
    pick_e_in,
    is_xy_in,
    is_corner_in,
    out,
    block,
    vectors_raw,
    values_raw,
    slot,
    x_local,
    x_middle,
    x_top,
    pick_z,
    pick_zt,
    pick_y,
    order,
    hat_xy,
    hat_xyt,
    hat_zw,
    pick_e,
    is_xy,
    is_corner,
    vectors,
    values,
    window,
    stage,
    solved,
    total,
    y_pack,
    c_pack,
    x_halo,
    y_halo,
    c_halo,
    x_rim,
    y_rim,
    c_rim,
    small,
    vertex_row,
    vertex_col,
    y_rows,
    sent,
    got_z,
    got_x,
    got_g,
    load_sem,
    halo_send,
    halo_recv,
    rim_send,
    rim_recv,
    sum_send,
    sum_recv,
    out_sem,
):
    group = lax.axis_index("group")
    dev = lax.axis_index("dev")
    n_low = min(8, n_dev)
    n_high = n_dev // n_low
    high, low = dev // n_low, dev % n_low

    def beside(step_x, step_y):
        return ((group + step_x + n_group) % n_group, (dev + step_y + n_dev) % n_dev)

    def came(step_x, step_y):
        from_x, from_y = group - step_x, dev - step_y
        return (from_x >= 0) & (from_x < n_group) & (from_y >= 0) & (from_y < n_dev)

    peers_z = [(group, high * n_low + (low + k) % n_low) for k in range(1, n_low)]
    peers_x = [(group, (high + k) % n_high * n_low + low) for k in range(1, n_high)]
    peers_g = [((group + k) % n_group, dev) for k in range(1, n_group)]

    pairs = [
        (residual, block.at[pl.ds(1, NX), pl.ds(0, NY), :]),
        (hat_xyt_in, hat_xyt),
        (hat_zw_in, hat_zw),
        (is_xy_in, is_xy),
        (slot_in, slot),
        (pick_e_in, pick_e),
        (is_corner_in, is_corner),
        (x_local_in, x_local),
        (x_middle_in, x_middle),
        (x_top_in, x_top),
        (vectors_in, vectors_raw),
        (values_in, values_raw),
        (order_in, order),
        (pick_z_in, pick_z),
        (pick_y_in, pick_y),
        (pick_zt_in, pick_zt),
        (hat_xy_in, hat_xy),
    ]
    loads = [
        pltpu.make_async_copy(source, target, load_sem.at[number])
        for number, (source, target) in enumerate(pairs)
    ]
    for load in loads:
        load.start()

    barrier = pltpu.get_barrier_semaphore()
    partners = [beside(*side) for side in SIDES] + peers_z + peers_x + peers_g
    for partner in partners:
        pl.semaphore_signal(barrier, inc=1, device_id=partner, device_id_type=MESH)

    rows = block.reshape(PLANES * ROWS, NZ)
    total_rows = total.reshape(PLANES * ROWS, NZ)
    empty = jnp.zeros((8, NZ), F32)
    for plane in range(PLANES):
        rows[plane * ROWS + 24 : plane * ROWS + 32, :] = empty

    def send_sides(source, x_planes, y_rows_at, x_into, y_into, c_into, send, recv):
        copies = []
        for number, (step_x, step_y) in enumerate(SIDES):
            plane = x_planes[step_x]
            row = y_rows_at[step_y]
            if step_y == 0:
                piece = source.at[pl.ds(plane * ROWS, 24), :]
                into = x_into.at[number]
            elif step_x == 0:
                for x in range(NX):
                    at = (x + 1) * ROWS + row
                    y_pack[number - 2, x : x + 1, :] = source[at : at + 1, :]
                piece = y_pack.at[number - 2]
                into = y_into.at[number - 2]
            else:
                c_pack[number - 4] = jnp.broadcast_to(
                    source[plane * ROWS + row : plane * ROWS + row + 1, :], (8, NZ)
                )
                piece = c_pack.at[number - 4]
                into = c_into.at[number - 4]
            copies.append(
                pltpu.make_async_remote_copy(
                    src_ref=piece,
                    dst_ref=into,
                    send_sem=send.at[number],
                    recv_sem=recv.at[number],
                    device_id=beside(step_x, step_y),
                    device_id_type=MESH,
                )
            )
        return copies

    loads[0].wait()
    halo = send_sides(
        rows, {1: 24, -1: 1, 0: 0}, {1: 23, -1: 0, 0: 0}, x_halo, y_halo, c_halo, halo_send, halo_recv
    )
    pl.semaphore_wait(barrier, len(partners))
    for copy in halo:
        copy.start()

    for load in loads[1:10]:
        load.wait()
    own_high, own_low = split(rows[ROWS : ROWS * (NX + 1), :])
    on_xy = mm(hat_xyt[...], own_high) + mm(hat_xyt[...], own_low)
    on_xy_high, on_xy_low = split(on_xy)
    on_vertex = mm(on_xy_high, hat_zw[...]) + mm(on_xy_low, hat_zw[...])
    at_vertex = jnp.sum(on_vertex * is_xy[...], axis=0, keepdims=True) * (1.0 / 1728.0)

    slots = slot[...]
    parts = jnp.concatenate([(slots >> 5).astype(F32), (slots & 31).astype(F32)], axis=0)
    picked = mm(parts.astype(BF16), pick_e[...])
    upper = jnp.sum(picked[0:8] * is_corner[...], axis=0, keepdims=True)
    lower = jnp.sum(picked[8:16] * is_corner[...], axis=0, keepdims=True)
    count = lax.broadcasted_iota(jnp.int32, (32, LANES), 0).astype(F32)
    is_upper = jnp.where(count == upper, 1.0, 0.0)
    is_lower = jnp.where(count == lower, 1.0, 0.0).astype(BF16)
    by_high, by_low = split(is_upper * at_vertex)
    small[...] = mm_t(by_high, is_lower) + mm_t(by_low, is_lower)

    eye = jnp.where(
        lax.broadcasted_iota(jnp.int32, (32, 32), 0) == lax.broadcasted_iota(jnp.int32, (32, 32), 1),
        1.0,
        0.0,
    )
    y_sums = [jnp.zeros((8, 128), F32) for _ in range(3)]
    for part in range(COARSE // 32):
        column = jnp.sum(small[part : part + 1, :] * eye, axis=1, keepdims=True)
        for level, factor in enumerate((x_local, x_middle, x_top)):
            weighted = column * factor[32 * part : 32 * part + 32, :]
            y_sums[level] = y_sums[level] + (
                (weighted[0:8] + weighted[8:16]) + (weighted[16:24] + weighted[24:32])
            )
    y_local, y_middle, y_top = [jnp.sum(value, axis=0, keepdims=True) for value in y_sums]
    row_number = lax.broadcasted_iota(jnp.int32, (8, 128), 0)
    y_rows[...] = jnp.broadcast_to(y_local, (8, 128))
    sent[0] = jnp.where(row_number == 0, y_middle, y_top)

    def send_sums(stage_number, peers, into, first):
        copies = []
        for k, peer in enumerate(peers):
            copies.append(
                pltpu.make_async_remote_copy(
                    src_ref=sent.at[stage_number],
                    dst_ref=into.at[k],
                    send_sem=sum_send.at[first + k],
                    recv_sem=sum_recv.at[first + k],
                    device_id=peer,
                    device_id_type=MESH,
                )
            )
        for copy in copies:
            copy.start()
        return copies

    def take_sums(copies, stage_number, into):
        for copy in copies:
            copy.wait()
        value = sent[stage_number]
        for k in range(len(copies)):
            value = value + into[k]
        return value

    first_sums = send_sums(0, peers_z, got_z, 0)

    for load in loads[10:]:
        load.wait()
    raw = jnp.concatenate([vectors_raw[...], values_raw[...]], axis=0)
    raw_high, raw_rest = split(raw)
    ordered = mm(raw_high, order[...]) + mm(raw_rest, order[...])
    for tile in range(3):
        vectors[tile] = ordered[0:192, 128 * tile : 128 * tile + 128]
        values[tile] = ordered[192:216, 128 * tile : 128 * tile + 128]

    for copy in halo:
        copy.wait()
    for number, (step_x, step_y) in enumerate(SIDES):
        inside = jnp.where(came(step_x, step_y), 1.0, 0.0)
        plane = {1: 0, -1: PLANES - 1}.get(step_x)
        row = {1: 24, -1: 25}.get(step_y)
        if step_y == 0:
            rows[plane * ROWS : plane * ROWS + 24, :] = x_halo[number] * inside
        elif step_x == 0:
            for x in range(NX):
                at = (x + 1) * ROWS + row
                rows[at : at + 1, :] = y_halo[number - 2, x : x + 1, :] * inside
        else:
            rows[plane * ROWS + row : plane * ROWS + row + 1, :] = (
                c_halo[number - 4, 0:1, :] * inside
            )

    lane = lax.broadcasted_iota(jnp.int32, (8, 128), 1)
    masks = [(lane >> (2 + bit)) & 1 == 1 for bit in range(3)]

    def make_windows(a, carry):
        planes = [
            rows[pl.ds(pl.multiple_of((6 * i + a) * ROWS, ROWS), ROWS), :] for i in range(BX)
        ]
        plane_high, plane_low = split(jnp.concatenate(planes, axis=0))
        along_high = mm_t(pick_z[...], plane_high).astype(BF16)
        along_low = mm_t(pick_z[...], plane_low).astype(BF16)
        picked = mm(along_high, pick_y[...]) + mm(along_low, pick_y[...])
        for tile in range(3):
            first = tile * 64
            pieces = swap_chunks(
                [picked[first + 8 * l : first + 8 * l + 8, :] for l in range(8)], masks
            )
            for b in range(8):
                window[tile, a, b] = pieces[b]
        return carry

    lax.fori_loop(0, 8, make_windows, 0)

    def bcast(ref, tile, row):
        return ref[tile, pl.ds(row, 8, stride=0), :]

    def solve(tile, carry):
        for b in (0, 4):
            fields = [window[tile, a, b : b + 4] for a in range(8)]
            for p in range(8):
                value = None
                for a in range(8):
                    term = bcast(vectors, tile, a * 8 + p) * fields[a]
                    value = term if value is None else value + term
                stage[p, b : b + 4] = value

        def middle(p, carry):
            fields = [stage[p, b] for b in range(8)]
            turned = []
            for q in range(8):
                value = None
                for b in range(8):
                    term = bcast(vectors, tile, 64 + b * 8 + q) * fields[b]
                    value = term if value is None else value + term
                turned.append(value)
            along = [vectors[tile, 128 + 8 * c : 136 + 8 * c, :] for c in range(8)]
            scale = bcast(values, tile, p) + values[tile, 16:24, :]
            divided = []
            for q in range(8):
                value = None
                for c in range(8):
                    term = along[c] * turned[q][c : c + 1, :]
                    value = term if value is None else value + term
                divided.append(value / (scale + bcast(values, tile, 8 + q)))
            across = [vectors[tile, pl.ds(128 + s, 8, stride=8), :] for s in range(8)]
            back = []
            for q in range(8):
                value = None
                for s in range(8):
                    term = across[s] * divided[q][s : s + 1, :]
                    value = term if value is None else value + term
                back.append(value)
            for b in range(8):
                value = None
                for q in range(8):
                    term = bcast(vectors, tile, 64 + b * 8 + q) * back[q]
                    value = term if value is None else value + term
                stage[p, b] = value
            return carry

        lax.fori_loop(0, 8, middle, 0)
        for b in (0, 4):
            fields = [stage[p, b : b + 4] for p in range(8)]
            for a in range(8):
                value = None
                for p in range(8):
                    term = bcast(vectors, tile, a * 8 + p) * fields[p]
                    value = term if value is None else value + term
                solved[tile, a, b : b + 4] = value
        return carry

    lax.fori_loop(0, 1, solve, 0)
    sent[1] = take_sums(first_sums, 0, got_z)
    second_sums = send_sums(1, peers_x, got_x, 8)
    lax.fori_loop(1, 2, solve, 0)
    row_sum = take_sums(second_sums, 1, got_x)
    sent[2] = row_sum
    third_sums = send_sums(2, peers_g, got_g, 16)
    lax.fori_loop(2, 3, solve, 0)
    y_all = take_sums(third_sums, 2, got_g)

    y_local = y_rows[0:1, :]
    y_middle = sent[2, 0:1, :]
    y_top = y_all[1:2, :]
    for part in range(COARSE // 32):
        here = slice(32 * part, 32 * part + 32)
        terms = x_local[here, :] * y_local + x_middle[here, :] * y_middle + x_top[here, :] * y_top
        column = jnp.sum(terms, axis=1, keepdims=True)
        vertex_col[part : part + 1, :] = jnp.sum(column * eye, axis=0, keepdims=True)
    vertex_col[20:32, :] = jnp.zeros((12, 32), F32)
    coarse_high, coarse_low = split(vertex_col[...])
    spread_out = mm(coarse_high, is_lower) + mm(coarse_low, is_lower)
    at_vertex = jnp.sum(spread_out * is_upper, axis=0, keepdims=True) * (1.0 / 1728.0)
    vertex_high, vertex_low = split(is_xy[...] * at_vertex)
    on_xy = mm_t(vertex_high, hat_zw[...]) + mm_t(vertex_low, hat_zw[...])
    vertex_row[...] = on_xy

    def add_up(a):
        pieces = []
        for tile in range(3):
            pieces.extend(swap_chunks([solved[tile, a, b] for b in range(8)], masks))
        piece_high, piece_low = split(jnp.concatenate(pieces, axis=0))
        along = mm(pick_zt[...], piece_high) + mm(pick_zt[...], piece_low)
        along_high, along_low = split(along)
        return mm_t(pick_y[...], along_high) + mm_t(pick_y[...], along_low)

    def store_sums(a, carry):
        value = add_up(a)
        for i in range(BX):
            total_rows[pl.ds(pl.multiple_of((6 * i + a) * ROWS, ROWS), ROWS), :] = value[
                32 * i : 32 * i + 32, :
            ]
        return carry

    lax.fori_loop(0, 6, store_sums, 0)
    for a in (6, 7):
        value = add_up(a)
        for i in range(BX):
            here = slice((6 * i + a) * ROWS, (6 * i + a + 1) * ROWS)
            piece = value[32 * i : 32 * i + 32, :]
            total_rows[here, :] = piece if i == BX - 1 else total_rows[here, :] + piece

    rim = send_sides(
        total_rows,
        {1: PLANES - 1, -1: 0, 0: 0},
        {1: 25, -1: 24, 0: 0},
        x_rim,
        y_rim,
        c_rim,
        rim_send,
        rim_recv,
    )
    for copy in rim:
        copy.start()

    field_high, field_low = split(vertex_row[...])
    field = mm(hat_xy[...], field_high) + mm(hat_xy[...], field_low)
    own = slice(ROWS, ROWS * (NX + 1))
    for x in range(NX):
        here = slice((x + 1) * ROWS, (x + 1) * ROWS + 24)
        total_rows[here, :] = total_rows[here, :] + field[x * ROWS : x * ROWS + 24, :]

    for copy in rim:
        copy.wait()
    for number, (step_x, step_y) in enumerate(SIDES):
        inside = jnp.where(came(step_x, step_y), 1.0, 0.0)
        plane = {1: 1, -1: PLANES - 2}.get(step_x)
        row = {1: 0, -1: 23}.get(step_y)
        if step_y == 0:
            here = slice(plane * ROWS, plane * ROWS + 24)
            total_rows[here, :] = total_rows[here, :] + x_rim[number] * inside
        elif step_x == 0:
            for x in range(NX):
                here = slice((x + 1) * ROWS + row, (x + 1) * ROWS + row + 1)
                total_rows[here, :] = total_rows[here, :] + y_rim[number - 2, x : x + 1, :] * inside
        else:
            here = slice(plane * ROWS + row, plane * ROWS + row + 1)
            total_rows[here, :] = total_rows[here, :] + c_rim[number - 4, 0:1, :] * inside

    store = pltpu.make_async_copy(total.at[pl.ds(1, NX), pl.ds(0, NY), :], out, out_sem)
    store.start()
    store.wait()


def local(residual, fdm_vectors, fdm_values, corner_slot, x_local, x_middle, x_top):
    n_group, n_dev = lax.axis_size("group"), lax.axis_size("dev")
    consts = tables()
    arguments = (
        residual,
        fdm_vectors.reshape(192, ELEMENTS),
        fdm_values.reshape(24, ELEMENTS),
        corner_slot,
        x_local,
        x_middle,
        x_top,
    ) + tuple(jnp.asarray(value) for value in consts)
    vmem = [pltpu.VMEM(value.shape, value.dtype) for value in arguments[1:]]
    n_sides = len(SIDES)
    scratch = (
        [pltpu.VMEM((PLANES, ROWS, NZ), F32)]
        + vmem
        + [
            pltpu.VMEM((3, 192, 128), F32),
            pltpu.VMEM((3, 24, 128), F32),
            pltpu.VMEM((3, 8, 8, 8, 128), F32),
            pltpu.VMEM((8, 8, 8, 128), F32),
            pltpu.VMEM((3, 8, 8, 8, 128), F32),
            pltpu.VMEM((PLANES, ROWS, NZ), F32),
            pltpu.VMEM((2, 24, NZ), F32),
            pltpu.VMEM((4, 8, NZ), F32),
            pltpu.VMEM((2, 24, NZ), F32),
            pltpu.VMEM((2, 24, NZ), F32),
            pltpu.VMEM((4, 8, NZ), F32),
            pltpu.VMEM((2, 24, NZ), F32),
            pltpu.VMEM((2, 24, NZ), F32),
            pltpu.VMEM((4, 8, NZ), F32),
            pltpu.VMEM((32, 32), F32),
            pltpu.VMEM((32, NZ), F32),
            pltpu.VMEM((32, 32), F32),
            pltpu.VMEM((8, 128), F32),
            pltpu.VMEM((3, 8, 128), F32),
            pltpu.VMEM((8, 8, 128), F32),
            pltpu.VMEM((8, 8, 128), F32),
            pltpu.VMEM((8, 8, 128), F32),
            pltpu.SemaphoreType.DMA((len(arguments),)),
            pltpu.SemaphoreType.DMA((n_sides,)),
            pltpu.SemaphoreType.DMA((n_sides,)),
            pltpu.SemaphoreType.DMA((n_sides,)),
            pltpu.SemaphoreType.DMA((n_sides,)),
            pltpu.SemaphoreType.DMA((24,)),
            pltpu.SemaphoreType.DMA((24,)),
            pltpu.SemaphoreType.DMA,
        ]
    )
    return pl.pallas_call(
        functools.partial(kernel, n_group, n_dev),
        out_shape=jax.ShapeDtypeStruct((NX, NY, NZ), F32),
        in_specs=[pl.BlockSpec(memory_space=pl.ANY)] * len(arguments),
        out_specs=pl.BlockSpec(memory_space=pl.ANY),
        scratch_shapes=scratch,
        compiler_params=pltpu.CompilerParams(
            collective_id=0, has_side_effects=True, vmem_limit_bytes=48 * 1024 * 1024
        ),
    )(*arguments)


def solution(mesh):
    return jax.shard_map(
        local,
        mesh=mesh,
        in_specs=(
            P("group", "dev", None),
            P(None, None, None, ("group", "dev")),
            P(None, None, ("group", "dev")),
            P(None, ("group", "dev")),
            P(("group", "dev"), None),
            P(("group", "dev"), None),
            P(("group", "dev"), None),
        ),
        out_specs=P("group", "dev", None),
        check_vma=False,
    )
```

profile of v0, /device:TPU:1, one launch (start us, length us, event | category | flops | bytes accessed | tf_op | source)
XLA Modules:
  0.0 55.8 jit_solution(10618184149719957248)
XLA Ops:
  0.0 0.0 copy-start.15
  0.0 0.7 %copy-done.15 = f32[8,640]{1,0:T(8,128)S(1)} copy-done((f32[8,640]{1,0:T(8,128)S(1)}, f32[8,640]{1,0:T(8,128)}, u32[]{:S(2)}) %copy-start.15) | copy-done | bytes 20504
  0.7 0.0 copy-start
  0.7 1.1 %copy-done = f32[24,24,144]{2,1,0:T(8,128)S(1)} copy-done((f32[24,24,144]{2,1,0:T(8,128)S(1)}, f32[24,24,144]{2,1,0:T(8,128)}, u32[]{:S(2)}) %copy-start) | copy-done | bytes 331800
  1.8 0.0 copy-start.1
  1.8 1.0 %copy-done.1 = bf16[384,640]{1,0:T(8,128)(2,1)S(1)} copy-done((bf16[384,640]{1,0:T(8,128)(2,1)S(1)}, bf16[384,640]{1,0:T(8,128)(2,1)}, u32[]{:S(2)}) %copy-start.1) | copy-done | bytes 491544
  2.8 0.0 copy-start.2
  2.8 1.0 %copy-done.2 = f32[640,128]{1,0:T(8,128)S(1)} copy-done((f32[640,128]{1,0:T(8,128)S(1)}, f32[640,128]{1,0:T(8,128)}, u32[]{:S(2)}) %copy-start.2) | copy-done | bytes 327704
  3.8 0.0 copy-start.3
  3.8 1.0 %copy-done.3 = f32[640,128]{1,0:T(8,128)S(1)} copy-done((f32[640,128]{1,0:T(8,128)S(1)}, f32[640,128]{1,0:T(8,128)}, u32[]{:S(2)}) %copy-start.3) | copy-done | bytes 327704
  4.8 0.0 copy-start.4
  4.8 1.0 %copy-done.4 = f32[640,128]{1,0:T(8,128)S(1)} copy-done((f32[640,128]{1,0:T(8,128)S(1)}, f32[640,128]{1,0:T(8,128)}, u32[]{:S(2)}) %copy-start.4) | copy-done | bytes 327704
  5.7 0.0 copy-start.5
  5.7 1.0 %copy-done.5 = f32[3,8,8,384]{3,2,1,0:T(8,128)S(1)} copy-done((f32[3,8,8,384]{3,2,1,0:T(8,128)S(1)}, f32[3,8,8,384]{3,2,1,0:T(8,128)}, u32[]{:S(2)}) %copy-start.5) | copy-done | bytes 294936
  6.7 1.0 %copy-done.6 = bf16[384,384]{1,0:T(8,128)(2,1)S(1)} copy-done((bf16[384,384]{1,0:T(8,128)(2,1)S(1)}, bf16[384,384]{1,0:T(8,128)(2,1)}, u32[]{:S(2)}) %copy-start.6) | copy-done | bytes 294936
  7.7 0.0 copy-start.7
  7.7 0.9 %copy-done.7 = bf16[768,32]{1,0:T(8,128)(2,1)S(1)} copy-done((bf16[768,32]{1,0:T(8,128)(2,1)S(1)}, bf16[768,32]{1,0:T(8,128)(2,1)}, u32[]{:S(2)}) %copy-start.7) | copy-done | bytes 49176
  8.6 0.0 copy-start.8
  8.6 0.9 %copy-done.8 = bf16[144,640]{1,0:T(8,128)(2,1)S(1)} copy-done((bf16[144,640]{1,0:T(8,128)(2,1)S(1)}, bf16[144,640]{1,0:T(8,128)(2,1)}, u32[]{:S(2)}) %copy-start.8) | copy-done | bytes 184344
  9.5 0.0 copy-start.9
  9.5 0.9 %copy-done.9 = bf16[192,144]{1,0:T(8,128)(2,1)S(1)} copy-done((bf16[192,144]{1,0:T(8,128)(2,1)S(1)}, bf16[192,144]{1,0:T(8,128)(2,1)}, u32[]{:S(2)}) %copy-start.9) | copy-done | bytes 55320
  10.4 0.0 copy-start.10
  10.4 0.9 %copy-done.10 = f32[32,640]{1,0:T(8,128)S(1)} copy-done((f32[32,640]{1,0:T(8,128)S(1)}, f32[32,640]{1,0:T(8,128)}, u32[]{:S(2)}) %copy-start.10) | copy-done | bytes 81944
  11.3 0.0 copy-start.11
  11.3 0.9 %copy-done.11 = bf16[144,192]{1,0:T(8,128)(2,1)S(1)} copy-done((bf16[144,192]{1,0:T(8,128)(2,1)S(1)}, bf16[144,192]{1,0:T(8,128)(2,1)}, u32[]{:S(2)}) %copy-start.11) | copy-done | bytes 55320
  12.2 0.0 copy-start.12
  12.2 0.8 %copy-done.12 = bf16[32,768]{1,0:T(8,128)(2,1)S(1)} copy-done((bf16[32,768]{1,0:T(8,128)(2,1)S(1)}, bf16[32,768]{1,0:T(8,128)(2,1)}, u32[]{:S(2)}) %copy-start.12) | copy-done | bytes 49176
  13.0 0.8 %copy-done.13 = f32[3,8,384]{2,1,0:T(8,128)S(1)} copy-done((f32[3,8,384]{2,1,0:T(8,128)S(1)}, f32[3,8,384]{2,1,0:T(8,128)}, u32[]{:S(2)}) %copy-start.13) | copy-done | bytes 36888
  13.8 0.8 %copy-done.14 = bf16[128,128]{1,0:T(8,128)(2,1)S(1)} copy-done((bf16[128,128]{1,0:T(8,128)(2,1)S(1)}, bf16[128,128]{1,0:T(8,128)(2,1)}, u32[]{:S(2)}) %copy-start.14) | copy-done | bytes 32792
  14.5 0.7 %copy-done.16 = s32[8,384]{1,0:T(8,128)S(1)} copy-done((s32[8,384]{1,0:T(8,128)S(1)}, s32[8,384]{1,0:T(8,128)}, u32[]{:S(2)}) %copy-start.16) | copy-done | bytes 12312
  15.2 39.8 %shard_map.163 = f32[24,24,144]{2,1,0:T(8,128)S(1)} custom-call(f32[24,24,144]{2,1,0:T(8,128)S(1)} %copy-done, f32[192,384]{1,0:T(8,128)S(1)} %bitcast.2, f32[24,384]{1,0:T(8,128)S(1)} %bitcast.3, s32[8,384]{1,0:T(8,128)S(1)} %copy-done.16, f32[640,128]{1,0:T(8,128)S(1)} %copy-done.2, f32[640,128]{1,0:T(8,128)S(1)} %copy-done.3, f32[640,128]{1,0:T(8,128)S(1)} %copy-done.4, ...), custom_call_target="tpu_custom_call" | custom-call | tf_op jit(solution)/shard_map/pallas_call | solution.py:592
  55.0 0.8 %copy.19 = f32[24,24,144]{2,1,0:T(8,128)} copy(f32[24,24,144]{2,1,0:T(8,128)S(1)} %shard_map.163) | data formatting | bytes 663552
  (4 shorter events, 0.0 us)
Async XLA Ops:
  0.0 0.7 %copy-start.15 = (f32[8,640]{1,0:T(8,128)S(1)}, f32[8,640]{1,0:T(8,128)}, u32[]{:S(2)}) copy-start(f32[8,640]{1,0:T(8,128)} %constant.29.clone.is_corner_in) | copy-start | bytes 61444
  0.7 1.1 %copy-start = (f32[24,24,144]{2,1,0:T(8,128)S(1)}, f32[24,24,144]{2,1,0:T(8,128)}, u32[]{:S(2)}) copy-start(f32[24,24,144]{2,1,0:T(8,128)} %residual.1) | copy-start | bytes 995332
  1.8 1.0 %copy-start.1 = (bf16[384,640]{1,0:T(8,128)(2,1)S(1)}, bf16[384,640]{1,0:T(8,128)(2,1)}, u32[]{:S(2)}) copy-start(bf16[384,640]{1,0:T(8,128)(2,1)} %constant.27.clone.pick_e_in) | copy-start | bytes 1474564
  2.8 1.0 %copy-start.2 = (f32[640,128]{1,0:T(8,128)S(1)}, f32[640,128]{1,0:T(8,128)}, u32[]{:S(2)}) copy-start(f32[640,128]{1,0:T(8,128)} %x_local_in.1) | copy-start | bytes 983044
  3.8 1.0 %copy-start.3 = (f32[640,128]{1,0:T(8,128)S(1)}, f32[640,128]{1,0:T(8,128)}, u32[]{:S(2)}) copy-start(f32[640,128]{1,0:T(8,128)} %x_middle_in.1) | copy-start | bytes 983044
  4.8 1.0 %copy-start.4 = (f32[640,128]{1,0:T(8,128)S(1)}, f32[640,128]{1,0:T(8,128)}, u32[]{:S(2)}) copy-start(f32[640,128]{1,0:T(8,128)} %x_top_in.1) | copy-start | bytes 983044
  5.7 1.0 %copy-start.5 = (f32[3,8,8,384]{3,2,1,0:T(8,128)S(1)}, f32[3,8,8,384]{3,2,1,0:T(8,128)}, u32[]{:S(2)}) copy-start(f32[3,8,8,384]{3,2,1,0:T(8,128)} %param.18) | copy-start | bytes 884740
  6.7 1.0 %copy-start.6 = (bf16[384,384]{1,0:T(8,128)(2,1)S(1)}, bf16[384,384]{1,0:T(8,128)(2,1)}, u32[]{:S(2)}) copy-start(bf16[384,384]{1,0:T(8,128)(2,1)} %constant.23.clone.order_in) | copy-start | bytes 884740
  7.7 0.9 %copy-start.7 = (bf16[768,32]{1,0:T(8,128)(2,1)S(1)}, bf16[768,32]{1,0:T(8,128)(2,1)}, u32[]{:S(2)}) copy-start(bf16[768,32]{1,0:T(8,128)(2,1)} %constant.24.clone.hat_xy_in) | copy-start | bytes 147460
  8.6 0.9 %copy-start.8 = (bf16[144,640]{1,0:T(8,128)(2,1)S(1)}, bf16[144,640]{1,0:T(8,128)(2,1)}, u32[]{:S(2)}) copy-start(bf16[144,640]{1,0:T(8,128)(2,1)} %constant.26.clone.hat_zw_in) | copy-start | bytes 552964
  9.5 0.9 %copy-start.9 = (bf16[192,144]{1,0:T(8,128)(2,1)S(1)}, bf16[192,144]{1,0:T(8,128)(2,1)}, u32[]{:S(2)}) copy-start(bf16[192,144]{1,0:T(8,128)(2,1)} %constant.20.clone.pick_z_in) | copy-start | bytes 165892
  10.4 0.9 %copy-start.10 = (f32[32,640]{1,0:T(8,128)S(1)}, f32[32,640]{1,0:T(8,128)}, u32[]{:S(2)}) copy-start(f32[32,640]{1,0:T(8,128)} %constant.28.clone.is_xy_in) | copy-start | bytes 245764
  11.3 0.9 %copy-start.11 = (bf16[144,192]{1,0:T(8,128)(2,1)S(1)}, bf16[144,192]{1,0:T(8,128)(2,1)}, u32[]{:S(2)}) copy-start(bf16[144,192]{1,0:T(8,128)(2,1)} %constant.21.clone.pick_zt_in) | copy-start | bytes 165892
  12.2 0.8 %copy-start.12 = (bf16[32,768]{1,0:T(8,128)(2,1)S(1)}, bf16[32,768]{1,0:T(8,128)(2,1)}, u32[]{:S(2)}) copy-start(bf16[32,768]{1,0:T(8,128)(2,1)} %constant.25.clone.hat_xyt_in) | copy-start | bytes 147460
  13.0 0.8 %copy-start.13 = (f32[3,8,384]{2,1,0:T(8,128)S(1)}, f32[3,8,384]{2,1,0:T(8,128)}, u32[]{:S(2)}) copy-start(f32[3,8,384]{2,1,0:T(8,128)} %param.19) | copy-start | bytes 110596
  13.8 0.8 %copy-start.14 = (bf16[128,128]{1,0:T(8,128)(2,1)S(1)}, bf16[128,128]{1,0:T(8,128)(2,1)}, u32[]{:S(2)}) copy-start(bf16[128,128]{1,0:T(8,128)(2,1)} %constant.22.clone.pick_y_in) | copy-start | bytes 98308
  14.5 0.7 %copy-start.16 = (s32[8,384]{1,0:T(8,128)S(1)}, s32[8,384]{1,0:T(8,128)}, u32[]{:S(2)}) copy-start(s32[8,384]{1,0:T(8,128)} %slot_in.1) | copy-start | bytes 36868
where the time goes:
time: 56.6 us; the launch traced here: 55.8 us
  Pallas kernels  39.8 us (70%)
  local copies, waits for them, and re-layouts  16 us (28%)
    pallas_call x1, Pallas kernels, local(): pl.pallas_call(functools.partial(kernel, n_group, n_dev), out_shape=jax.S...  39.8 us
    unnamed x35, local copies, waits for them, and re-layouts  16 us

commit v1 on v0

--- a/solution.py
+++ b/solution.py
@@ -596,7 +596,7 @@
         out_specs=pl.BlockSpec(memory_space=pl.ANY),
         scratch_shapes=scratch,
         compiler_params=pltpu.CompilerParams(
-            collective_id=0, has_side_effects=True, vmem_limit_bytes=48 * 1024 * 1024
+            collective_id=0, has_side_effects=True, vmem_limit_bytes=56 * 1024 * 1024
         ),
     )(*arguments)
 

time: 56.6 us -> 40.7 us (0.72); the launches traced: 55.8 us -> 40.6 us
  local copies, waits for them, and re-layouts: 16 us -> 1.92 us
  Pallas kernels: 39.8 us -> 38.6 us
    unnamed x35 -> x1, local copies, waits for them, and re-layouts: 16 us -> 1.92 us
    pallas_call x1, Pallas kernels: 39.8 us -> 38.6 us  [local(): pl.pallas_call(functools.partial(kernel, n_group, n_dev), out_shape=jax.S...]
where the time goes in v1:
time: 40.7 us; the launch traced here: 40.6 us
  Pallas kernels  38.6 us (95%)
  local copies, waits for them, and re-layouts  1.92 us (5%)
    pallas_call x1, Pallas kernels, local(): pl.pallas_call(functools.partial(kernel, n_group, n_dev), out_shape=jax.S...  38.6 us
    unnamed x1, local copies, waits for them, and re-layouts  1.92 us

profile of v1, /device:TPU:1, one launch (start us, length us, event | category | flops | bytes accessed | tf_op | source)
XLA Modules:
  0.0 40.6 jit_solution(15825437401150468263)
XLA Ops:
  0.0 38.6 %shard_map.163 = f32[24,24,144]{2,1,0:T(8,128)} custom-call(f32[24,24,144]{2,1,0:T(8,128)} %residual.1, f32[192,384]{1,0:T(8,128)} %bitcast.2, f32[24,384]{1,0:T(8,128)} %bitcast.3, s32[8,384]{1,0:T(8,128)} %slot_in.1, f32[640,128]{1,0:T(8,128)} %x_local_in.1, f32[640,128]{1,0:T(8,128)} %x_middle_in.1, f32[640,128]{1,0:T(8,128)} %x_top_in.1, ...), custom_call_target="tpu_custom_call" | custom-call | tf_op jit(solution)/shard_map/pallas_call | solution.py:592
  38.6 1.9 %copy.19 = f32[24,24,144]{2,1,0:T(8,128)} copy(f32[24,24,144]{2,1,0:T(8,128)} %shard_map.163) | data formatting | bytes 663552

commit v2 on v1

--- a/solution.py
+++ b/solution.py
@@ -180,7 +180,6 @@
     rim_recv,
     sum_send,
     sum_recv,
-    out_sem,
 ):
     group = lax.axis_index("group")
     dev = lax.axis_index("dev")
@@ -386,7 +385,7 @@
                 window[tile, a, b] = pieces[b]
         return carry
 
-    lax.fori_loop(0, 8, make_windows, 0)
+    lax.fori_loop(0, 8, make_windows, 0, unroll=8)
 
     def bcast(ref, tile, row):
         return ref[tile, pl.ds(row, 8, stride=0), :]
@@ -489,7 +488,7 @@
             ]
         return carry
 
-    lax.fori_loop(0, 6, store_sums, 0)
+    lax.fori_loop(0, 6, store_sums, 0, unroll=6)
     for a in (6, 7):
         value = add_up(a)
         for i in range(BX):
@@ -512,31 +511,25 @@
 
     field_high, field_low = split(vertex_row[...])
     field = mm(hat_xy[...], field_high) + mm(hat_xy[...], field_low)
-    own = slice(ROWS, ROWS * (NX + 1))
     for x in range(NX):
-        here = slice((x + 1) * ROWS, (x + 1) * ROWS + 24)
-        total_rows[here, :] = total_rows[here, :] + field[x * ROWS : x * ROWS + 24, :]
+        at = (x + 1) * ROWS
+        out[x] = total_rows[at : at + NY, :] + field[x * ROWS : x * ROWS + NY, :]
 
     for copy in rim:
         copy.wait()
     for number, (step_x, step_y) in enumerate(SIDES):
         inside = jnp.where(came(step_x, step_y), 1.0, 0.0)
-        plane = {1: 1, -1: PLANES - 2}.get(step_x)
-        row = {1: 0, -1: 23}.get(step_y)
+        x = {1: 0, -1: NX - 1}.get(step_x)
+        y = {1: 0, -1: NY - 1}.get(step_y)
         if step_y == 0:
-            here = slice(plane * ROWS, plane * ROWS + 24)
-            total_rows[here, :] = total_rows[here, :] + x_rim[number] * inside
+            out[x] = out[x] + x_rim[number] * inside
         elif step_x == 0:
             for x in range(NX):
-                here = slice((x + 1) * ROWS + row, (x + 1) * ROWS + row + 1)
-                total_rows[here, :] = total_rows[here, :] + y_rim[number - 2, x : x + 1, :] * inside
+                out[x, y : y + 1, :] = (
+                    out[x, y : y + 1, :] + y_rim[number - 2, x : x + 1, :] * inside
+                )
         else:
-            here = slice(plane * ROWS + row, plane * ROWS + row + 1)
-            total_rows[here, :] = total_rows[here, :] + c_rim[number - 4, 0:1, :] * inside
-
-    store = pltpu.make_async_copy(total.at[pl.ds(1, NX), pl.ds(0, NY), :], out, out_sem)
-    store.start()
-    store.wait()
+            out[x, y : y + 1, :] = out[x, y : y + 1, :] + c_rim[number - 4, 0:1, :] * inside
 
 
 def local(residual, fdm_vectors, fdm_values, corner_slot, x_local, x_middle, x_top):
@@ -586,19 +579,18 @@
             pltpu.SemaphoreType.DMA((n_sides,)),
             pltpu.SemaphoreType.DMA((24,)),
             pltpu.SemaphoreType.DMA((24,)),
-            pltpu.SemaphoreType.DMA,
         ]
     )
     return pl.pallas_call(
         functools.partial(kernel, n_group, n_dev),
-        out_shape=jax.ShapeDtypeStruct((NX, NY, NZ), F32),
+        out_shape=pltpu.VMEM((NX, NY, NZ), F32),
         in_specs=[pl.BlockSpec(memory_space=pl.ANY)] * len(arguments),
-        out_specs=pl.BlockSpec(memory_space=pl.ANY),
+        out_specs=pl.BlockSpec(memory_space=pltpu.VMEM),
         scratch_shapes=scratch,
         compiler_params=pltpu.CompilerParams(
-            collective_id=0, has_side_effects=True, vmem_limit_bytes=56 * 1024 * 1024
+            collective_id=0, has_side_effects=True, vmem_limit_bytes=40 * 1024 * 1024
         ),
-    )(*arguments)
+    )(*[pltpu.with_memory_space_constraint(value, pltpu.HBM) for value in arguments])
 
 
 def solution(mesh):

time: 40.7 us -> 33.2 us (0.82)
  Pallas kernels: 38.6 us -> 32.3 us
  local copies, waits for them, and re-layouts: 1.92 us -> 0.82 us
    pallas_call x1, Pallas kernels: 38.6 us -> 32.3 us  [local(): pl.pallas_call(functools.partial(kernel, n_group, n_dev), out_shape=pltpu...]
    unnamed x1, local copies, waits for them, and re-layouts: 1.92 us -> 0.82 us
where the time goes in v2:
time: 33.2 us
  Pallas kernels  32.3 us (97%)
  local copies, waits for them, and re-layouts  0.82 us (2%)
    pallas_call x1, Pallas kernels, local(): pl.pallas_call(functools.partial(kernel, n_group, n_dev), out_shape=pltpu...  32.3 us
    unnamed x1, local copies, waits for them, and re-layouts  0.82 us

profile of v2, /device:TPU:1, one launch (start us, length us, event | category | flops | bytes accessed | tf_op | source)
XLA Modules:
  0.0 33.2 jit_solution(9262868095352276860)
XLA Ops:
  0.0 32.3 %shard_map.163 = f32[24,24,144]{2,1,0:T(8,128)S(1)} custom-call(f32[24,24,144]{2,1,0:T(8,128)} %residual.1, f32[192,384]{1,0:T(8,128)} %bitcast.2, f32[24,384]{1,0:T(8,128)} %bitcast.3, s32[8,384]{1,0:T(8,128)} %slot_in.1, f32[640,128]{1,0:T(8,128)} %x_local_in.1, f32[640,128]{1,0:T(8,128)} %x_middle_in.1, f32[640,128]{1,0:T(8,128)} %x_top_in.1, ...), custom_call_target="tpu_custom_call" | custom-call | tf_op jit(solution)/shard_map/pallas_call | solution.py:584
  32.4 0.8 %copy.19 = f32[24,24,144]{2,1,0:T(8,128)} copy(f32[24,24,144]{2,1,0:T(8,128)S(1)} %shard_map.163) | data formatting | bytes 663552

commit v3 on v2

--- a/solution.py
+++ b/solution.py
@@ -74,7 +74,8 @@
     return (
         pick_z.astype(bf16),
         pick_z.T.copy().astype(bf16),
-        pick_y.astype(bf16),
+        np.concatenate([pick_y, pick_y], axis=0).astype(bf16),
+        np.concatenate([pick_y, pick_y], axis=1).astype(bf16),
         order.astype(bf16),
         hat_xy.astype(bf16),
         hat_xy.T.copy().astype(bf16),
@@ -126,6 +127,7 @@
     pick_z_in,
     pick_zt_in,
     pick_y_in,
+    pick_yt_in,
     order_in,
     hat_xy_in,
     hat_xyt_in,
@@ -144,6 +146,7 @@
     pick_z,
     pick_zt,
     pick_y,
+    pick_yt,
     order,
     hat_xy,
     hat_xyt,
@@ -166,7 +169,6 @@
     y_rim,
     c_rim,
     small,
-    vertex_row,
     vertex_col,
     y_rows,
     sent,
@@ -214,6 +216,7 @@
         (order_in, order),
         (pick_z_in, pick_z),
         (pick_y_in, pick_y),
+        (pick_yt_in, pick_yt),
         (pick_zt_in, pick_zt),
         (hat_xy_in, hat_xy),
     ]
@@ -372,10 +375,9 @@
         planes = [
             rows[pl.ds(pl.multiple_of((6 * i + a) * ROWS, ROWS), ROWS), :] for i in range(BX)
         ]
-        plane_high, plane_low = split(jnp.concatenate(planes, axis=0))
-        along_high = mm_t(pick_z[...], plane_high).astype(BF16)
-        along_low = mm_t(pick_z[...], plane_low).astype(BF16)
-        picked = mm(along_high, pick_y[...]) + mm(along_low, pick_y[...])
+        both = jnp.concatenate(split(jnp.concatenate(planes, axis=0)), axis=0)
+        along = mm_t(pick_z[...], both).astype(BF16)
+        picked = mm(along, pick_y[...])
         for tile in range(3):
             first = tile * 64
             pieces = swap_chunks(
@@ -453,6 +455,44 @@
     sent[2] = row_sum
     third_sums = send_sums(2, peers_g, got_g, 16)
     lax.fori_loop(2, 3, solve, 0)
+    def add_up(a):
+        pieces = []
+        for tile in range(3):
+            pieces.extend(swap_chunks([solved[tile, a, b] for b in range(8)], masks))
+        both = jnp.concatenate(split(jnp.concatenate(pieces, axis=0)), axis=1)
+        along = mm(pick_zt[...], both)
+        along = along[:, 0:128] + along[:, 128:256]
+        return mm_t(pick_yt[...], jnp.concatenate(split(along), axis=1))
+
+    def store_sums(a, carry):
+        value = add_up(a)
+        for i in range(BX):
+            total_rows[pl.ds(pl.multiple_of((6 * i + a) * ROWS, ROWS), ROWS), :] = value[
+                32 * i : 32 * i + 32, :
+            ]
+        return carry
+
+    lax.fori_loop(0, 6, store_sums, 0, unroll=6)
+    for a in (6, 7):
+        value = add_up(a)
+        for i in range(BX):
+            here = slice((6 * i + a) * ROWS, (6 * i + a + 1) * ROWS)
+            piece = value[32 * i : 32 * i + 32, :]
+            total_rows[here, :] = piece if i == BX - 1 else total_rows[here, :] + piece
+
+    rim = send_sides(
+        total_rows,
+        {1: PLANES - 1, -1: 0, 0: 0},
+        {1: 25, -1: 24, 0: 0},
+        x_rim,
+        y_rim,
+        c_rim,
+        rim_send,
+        rim_recv,
+    )
+    for copy in rim:
+        copy.start()
+
     y_all = take_sums(third_sums, 2, got_g)
 
     y_local = y_rows[0:1, :]
@@ -469,47 +509,7 @@
     at_vertex = jnp.sum(spread_out * is_upper, axis=0, keepdims=True) * (1.0 / 1728.0)
     vertex_high, vertex_low = split(is_xy[...] * at_vertex)
     on_xy = mm_t(vertex_high, hat_zw[...]) + mm_t(vertex_low, hat_zw[...])
-    vertex_row[...] = on_xy
-
-    def add_up(a):
-        pieces = []
-        for tile in range(3):
-            pieces.extend(swap_chunks([solved[tile, a, b] for b in range(8)], masks))
-        piece_high, piece_low = split(jnp.concatenate(pieces, axis=0))
-        along = mm(pick_zt[...], piece_high) + mm(pick_zt[...], piece_low)
-        along_high, along_low = split(along)
-        return mm_t(pick_y[...], along_high) + mm_t(pick_y[...], along_low)
-
-    def store_sums(a, carry):
-        value = add_up(a)
-        for i in range(BX):
-            total_rows[pl.ds(pl.multiple_of((6 * i + a) * ROWS, ROWS), ROWS), :] = value[
-                32 * i : 32 * i + 32, :
-            ]
-        return carry
-
-    lax.fori_loop(0, 6, store_sums, 0, unroll=6)
-    for a in (6, 7):
-        value = add_up(a)
-        for i in range(BX):
-            here = slice((6 * i + a) * ROWS, (6 * i + a + 1) * ROWS)
-            piece = value[32 * i : 32 * i + 32, :]
-            total_rows[here, :] = piece if i == BX - 1 else total_rows[here, :] + piece
-
-    rim = send_sides(
-        total_rows,
-        {1: PLANES - 1, -1: 0, 0: 0},
-        {1: 25, -1: 24, 0: 0},
-        x_rim,
-        y_rim,
-        c_rim,
-        rim_send,
-        rim_recv,
-    )
-    for copy in rim:
-        copy.start()
-
-    field_high, field_low = split(vertex_row[...])
+    field_high, field_low = split(on_xy)
     field = mm(hat_xy[...], field_high) + mm(hat_xy[...], field_low)
     for x in range(NX):
         at = (x + 1) * ROWS
@@ -565,7 +565,6 @@
             pltpu.VMEM((2, 24, NZ), F32),
             pltpu.VMEM((4, 8, NZ), F32),
             pltpu.VMEM((32, 32), F32),
-            pltpu.VMEM((32, NZ), F32),
             pltpu.VMEM((32, 32), F32),
             pltpu.VMEM((8, 128), F32),
             pltpu.VMEM((3, 8, 128), F32),

time: 33.2 us -> 29.1 us (0.88)
  Pallas kernels: 32.3 us -> 28.2 us
    pallas_call x1, Pallas kernels: 32.3 us -> 28.2 us  [local(): pl.pallas_call(functools.partial(kernel, n_group, n_dev), out_shape=pltpu...]
where the time goes in v3:
time: 29.1 us; the launch traced here: 29 us
  Pallas kernels  28.2 us (97%)
  local copies, waits for them, and re-layouts  0.82 us (3%)
    pallas_call x1, Pallas kernels, local(): pl.pallas_call(functools.partial(kernel, n_group, n_dev), out_shape=pltpu...  28.2 us
    unnamed x1, local copies, waits for them, and re-layouts  0.82 us

profile of v3, /device:TPU:1, one launch (start us, length us, event | category | flops | bytes accessed | tf_op | source)
XLA Modules:
  0.0 29.0 jit_solution(9979345253407077333)
XLA Ops:
  0.0 28.2 %shard_map.172 = f32[24,24,144]{2,1,0:T(8,128)S(1)} custom-call(f32[24,24,144]{2,1,0:T(8,128)} %residual.1, f32[192,384]{1,0:T(8,128)} %bitcast.2, f32[24,384]{1,0:T(8,128)} %bitcast.3, s32[8,384]{1,0:T(8,128)} %slot_in.1, f32[640,128]{1,0:T(8,128)} %x_local_in.1, f32[640,128]{1,0:T(8,128)} %x_middle_in.1, f32[640,128]{1,0:T(8,128)} %x_top_in.1, ...), custom_call_target="tpu_custom_call" | custom-call | tf_op jit(solution)/shard_map/pallas_call | solution.py:583
  28.2 0.8 %copy.20 = f32[24,24,144]{2,1,0:T(8,128)} copy(f32[24,24,144]{2,1,0:T(8,128)S(1)} %shard_map.172) | data formatting | bytes 663552

commit v4 on v3

--- a/solution.py
+++ b/solution.py
@@ -160,8 +160,10 @@
     stage,
     solved,
     total,
-    y_pack,
-    c_pack,
+    y_halo_pack,
+    c_halo_pack,
+    y_rim_pack,
+    c_rim_pack,
     x_halo,
     y_halo,
     c_halo,
@@ -196,6 +198,9 @@
         from_x, from_y = group - step_x, dev - step_y
         return (from_x >= 0) & (from_x < n_group) & (from_y >= 0) & (from_y < n_dev)
 
+    def goes(step_x, step_y):
+        return came(-step_x, -step_y)
+
     peers_z = [(group, high * n_low + (low + k) % n_low) for k in range(1, n_low)]
     peers_x = [(group, (high + k) % n_high * n_low + low) for k in range(1, n_high)]
     peers_g = [((group + k) % n_group, dev) for k in range(1, n_group)]
@@ -228,7 +233,15 @@
         load.start()
 
     barrier = pltpu.get_barrier_semaphore()
-    partners = [beside(*side) for side in SIDES] + peers_z + peers_x + peers_g
+    partners = peers_z + peers_x + peers_g
+    greeted = len(partners)
+    for side in SIDES:
+        greeted = greeted + goes(*side).astype(jnp.int32)
+
+        @pl.when(goes(*side))
+        def _(side=side):
+            pl.semaphore_signal(barrier, inc=1, device_id=beside(*side), device_id_type=MESH)
+
     for partner in partners:
         pl.semaphore_signal(barrier, inc=1, device_id=partner, device_id_type=MESH)
 
@@ -236,10 +249,12 @@
     total_rows = total.reshape(PLANES * ROWS, NZ)
     empty = jnp.zeros((8, NZ), F32)
     for plane in range(PLANES):
-        rows[plane * ROWS + 24 : plane * ROWS + 32, :] = empty
-
-    def send_sides(source, x_planes, y_rows_at, x_into, y_into, c_into, send, recv):
+        for part in range(0 if plane in (0, PLANES - 1) else 24, ROWS, 8):
+            rows[plane * ROWS + part : plane * ROWS + part + 8, :] = empty
+
+    def send_sides(source, x_planes, y_rows_at, packs, x_into, y_into, c_into, send, recv):
         copies = []
+        y_pack, c_pack = packs
         for number, (step_x, step_y) in enumerate(SIDES):
             plane = x_planes[step_x]
             row = y_rows_at[step_y]
@@ -253,9 +268,7 @@
                 piece = y_pack.at[number - 2]
                 into = y_into.at[number - 2]
             else:
-                c_pack[number - 4] = jnp.broadcast_to(
-                    source[plane * ROWS + row : plane * ROWS + row + 1, :], (8, NZ)
-                )
+                c_pack[number - 4] = source[plane * ROWS + row : plane * ROWS + row + 1, :]
                 piece = c_pack.at[number - 4]
                 into = c_into.at[number - 4]
             copies.append(
@@ -272,11 +285,23 @@
 
     loads[0].wait()
     halo = send_sides(
-        rows, {1: 24, -1: 1, 0: 0}, {1: 23, -1: 0, 0: 0}, x_halo, y_halo, c_halo, halo_send, halo_recv
+        rows,
+        {1: 24, -1: 1, 0: 0},
+        {1: 23, -1: 0, 0: 0},
+        (y_halo_pack, c_halo_pack),
+        x_halo,
+        y_halo,
+        c_halo,
+        halo_send,
+        halo_recv,
     )
-    pl.semaphore_wait(barrier, len(partners))
-    for copy in halo:
-        copy.start()
+    pl.semaphore_wait(barrier, greeted)
+
+    def start_sides(copies):
+        for side, copy in zip(SIDES, copies):
+            pl.when(goes(*side))(copy.start)
+
+    start_sides(halo)
 
     for load in loads[1:10]:
         load.wait()
@@ -334,7 +359,7 @@
 
     def take_sums(copies, stage_number, into):
         for copy in copies:
-            copy.wait()
+            copy.wait_recv()
         value = sent[stage_number]
         for k in range(len(copies)):
             value = value + into[k]
@@ -351,22 +376,21 @@
         vectors[tile] = ordered[0:192, 128 * tile : 128 * tile + 128]
         values[tile] = ordered[192:216, 128 * tile : 128 * tile + 128]
 
-    for copy in halo:
-        copy.wait()
     for number, (step_x, step_y) in enumerate(SIDES):
-        inside = jnp.where(came(step_x, step_y), 1.0, 0.0)
         plane = {1: 0, -1: PLANES - 1}.get(step_x)
         row = {1: 24, -1: 25}.get(step_y)
-        if step_y == 0:
-            rows[plane * ROWS : plane * ROWS + 24, :] = x_halo[number] * inside
-        elif step_x == 0:
-            for x in range(NX):
-                at = (x + 1) * ROWS + row
-                rows[at : at + 1, :] = y_halo[number - 2, x : x + 1, :] * inside
-        else:
-            rows[plane * ROWS + row : plane * ROWS + row + 1, :] = (
-                c_halo[number - 4, 0:1, :] * inside
-            )
+
+        @pl.when(came(step_x, step_y))
+        def _(number=number, step_x=step_x, step_y=step_y, plane=plane, row=row):
+            halo[number].wait_recv()
+            if step_y == 0:
+                rows[plane * ROWS : plane * ROWS + 24, :] = x_halo[number]
+            elif step_x == 0:
+                for x in range(NX):
+                    at = (x + 1) * ROWS + row
+                    rows[at : at + 1, :] = y_halo[number - 2, x : x + 1, :]
+            else:
+                rows[plane * ROWS + row : plane * ROWS + row + 1, :] = c_halo[number - 4]
 
     lane = lax.broadcasted_iota(jnp.int32, (8, 128), 1)
     masks = [(lane >> (2 + bit)) & 1 == 1 for bit in range(3)]
@@ -451,10 +475,9 @@
     sent[1] = take_sums(first_sums, 0, got_z)
     second_sums = send_sums(1, peers_x, got_x, 8)
     lax.fori_loop(1, 2, solve, 0)
-    row_sum = take_sums(second_sums, 1, got_x)
-    sent[2] = row_sum
+    lax.fori_loop(2, 3, solve, 0)
+    sent[2] = take_sums(second_sums, 1, got_x)
     third_sums = send_sums(2, peers_g, got_g, 16)
-    lax.fori_loop(2, 3, solve, 0)
     def add_up(a):
         pieces = []
         for tile in range(3):
@@ -484,14 +507,14 @@
         total_rows,
         {1: PLANES - 1, -1: 0, 0: 0},
         {1: 25, -1: 24, 0: 0},
+        (y_rim_pack, c_rim_pack),
         x_rim,
         y_rim,
         c_rim,
         rim_send,
         rim_recv,
     )
-    for copy in rim:
-        copy.start()
+    start_sides(rim)
 
     y_all = take_sums(third_sums, 2, got_g)
 
@@ -515,21 +538,30 @@
         at = (x + 1) * ROWS
         out[x] = total_rows[at : at + NY, :] + field[x * ROWS : x * ROWS + NY, :]
 
-    for copy in rim:
-        copy.wait()
     for number, (step_x, step_y) in enumerate(SIDES):
-        inside = jnp.where(came(step_x, step_y), 1.0, 0.0)
         x = {1: 0, -1: NX - 1}.get(step_x)
         y = {1: 0, -1: NY - 1}.get(step_y)
-        if step_y == 0:
-            out[x] = out[x] + x_rim[number] * inside
-        elif step_x == 0:
-            for x in range(NX):
-                out[x, y : y + 1, :] = (
-                    out[x, y : y + 1, :] + y_rim[number - 2, x : x + 1, :] * inside
-                )
-        else:
-            out[x, y : y + 1, :] = out[x, y : y + 1, :] + c_rim[number - 4, 0:1, :] * inside
+
+        @pl.when(came(step_x, step_y))
+        def _(number=number, step_x=step_x, step_y=step_y, x=x, y=y):
+            rim[number].wait_recv()
+            if step_y == 0:
+                out[x] = out[x] + x_rim[number]
+            elif step_x == 0:
+                for x in range(NX):
+                    out[x, y : y + 1, :] = out[x, y : y + 1, :] + y_rim[number - 2, x : x + 1, :]
+            else:
+                out[x, y : y + 1, :] = out[x, y : y + 1, :] + c_rim[number - 4]
+
+    for side, halo_copy, rim_copy in zip(SIDES, halo, rim):
+
+        @pl.when(goes(*side))
+        def _(halo_copy=halo_copy, rim_copy=rim_copy):
+            halo_copy.wait_send()
+            rim_copy.wait_send()
+
+    for copy in first_sums + second_sums + third_sums:
+        copy.wait_send()
 
 
 def local(residual, fdm_vectors, fdm_values, corner_slot, x_local, x_middle, x_top):
@@ -557,13 +589,15 @@
             pltpu.VMEM((3, 8, 8, 8, 128), F32),
             pltpu.VMEM((PLANES, ROWS, NZ), F32),
             pltpu.VMEM((2, 24, NZ), F32),
-            pltpu.VMEM((4, 8, NZ), F32),
+            pltpu.VMEM((4, 1, NZ), F32),
+            pltpu.VMEM((2, 24, NZ), F32),
+            pltpu.VMEM((4, 1, NZ), F32),
             pltpu.VMEM((2, 24, NZ), F32),
             pltpu.VMEM((2, 24, NZ), F32),
-            pltpu.VMEM((4, 8, NZ), F32),
+            pltpu.VMEM((4, 1, NZ), F32),
             pltpu.VMEM((2, 24, NZ), F32),
             pltpu.VMEM((2, 24, NZ), F32),
-            pltpu.VMEM((4, 8, NZ), F32),
+            pltpu.VMEM((4, 1, NZ), F32),
             pltpu.VMEM((32, 32), F32),
             pltpu.VMEM((32, 32), F32),
             pltpu.VMEM((8, 128), F32),

time: 29.1 us -> 26.3 us (0.904)
  Pallas kernels: 28.2 us -> 25.4 us
    pallas_call x1, Pallas kernels: 28.2 us -> 25.4 us  [local(): pl.pallas_call(functools.partial(kernel, n_group, n_dev), out_shape=pltpu...]
where the time goes in v4:
time: 26.3 us; the launch traced here: 26.2 us
  Pallas kernels  25.4 us (97%)
  local copies, waits for them, and re-layouts  0.82 us (3%)
    pallas_call x1, Pallas kernels, local(): pl.pallas_call(functools.partial(kernel, n_group, n_dev), out_shape=pltpu...  25.4 us
    unnamed x1, local copies, waits for them, and re-layouts  0.82 us

profile of v4, /device:TPU:1, one launch (start us, length us, event | category | flops | bytes accessed | tf_op | source)
XLA Modules:
  0.0 26.2 jit_solution(15046785224434074713)
XLA Ops:
  0.0 25.4 %shard_map.172 = f32[24,24,144]{2,1,0:T(8,128)S(1)} custom-call(f32[24,24,144]{2,1,0:T(8,128)} %residual.1, f32[192,384]{1,0:T(8,128)} %bitcast.2, f32[24,384]{1,0:T(8,128)} %bitcast.3, s32[8,384]{1,0:T(8,128)} %slot_in.1, f32[640,128]{1,0:T(8,128)} %x_local_in.1, f32[640,128]{1,0:T(8,128)} %x_middle_in.1, f32[640,128]{1,0:T(8,128)} %x_top_in.1, ...), custom_call_target="tpu_custom_call" | custom-call | tf_op jit(solution)/shard_map/pallas_call | solution.py:617
  25.4 0.8 %copy.20 = f32[24,24,144]{2,1,0:T(8,128)} copy(f32[24,24,144]{2,1,0:T(8,128)S(1)} %shard_map.172) | data formatting | bytes 663552

commit v5 on v4

--- a/solution.py
+++ b/solution.py
@@ -174,25 +174,32 @@
     vertex_col,
     y_rows,
     sent,
-    got_z,
-    got_x,
-    got_g,
+    got_first,
+    got_second,
     load_sem,
     halo_send,
     halo_recv,
     rim_send,
     rim_recv,
-    sum_send,
-    sum_recv,
+    first_send,
+    first_recv,
+    second_send,
+    second_recv,
+    hello,
 ):
     group = lax.axis_index("group")
     dev = lax.axis_index("dev")
-    n_low = min(8, n_dev)
-    n_high = n_dev // n_low
-    high, low = dev // n_low, dev % n_low
+    n_z = min(8, n_dev)
+    n_x, n_y = n_dev // n_z, n_group // 2
+    at_x, at_z = dev // n_z, dev % n_z
+    at_y, core = group // 2, group % 2
 
     def beside(step_x, step_y):
-        return ((group + step_x + n_group) % n_group, (dev + step_y + n_dev) % n_dev)
+        return (group + step_x, dev + step_y)
+
+    def ahead(place, step, size):
+        place = place + step
+        return jnp.where(place >= size, place - size, place)
 
     def came(step_x, step_y):
         from_x, from_y = group - step_x, dev - step_y
@@ -201,9 +208,25 @@
     def goes(step_x, step_y):
         return came(-step_x, -step_y)
 
-    peers_z = [(group, high * n_low + (low + k) % n_low) for k in range(1, n_low)]
-    peers_x = [(group, (high + k) % n_high * n_low + low) for k in range(1, n_high)]
-    peers_g = [((group + k) % n_group, dev) for k in range(1, n_group)]
+    peers_first, peers_second = [], []
+    for step in range(n_z):
+        for other in range(2):
+            if step or other:
+                to_z = ahead(at_z, step, n_z)
+                to_core = 1 - core if other else core
+                device = (2 * at_y + to_core, n_z * at_x + to_z)
+                later = 2 * to_z + to_core > 2 * at_z + core
+                peers_first.append((other == 0, device, later))
+    for step in range(n_x):
+        for other in range(n_y):
+            if step or other:
+                to_x, to_y = ahead(at_x, step, n_x), ahead(at_y, other, n_y)
+                device = (2 * to_y + core, n_z * to_x + at_z)
+                later = n_y * to_x + to_y > n_y * at_x + at_y
+                peers_second.append((other == 0, device, later))
+    earlier_first = 2 * at_z + core
+    earlier_second = n_y * at_x + at_y
+    middle_z = (at_z >= 1) & (at_z <= 3)
 
     pairs = [
         (residual, block.at[pl.ds(1, NX), pl.ds(0, NY), :]),
@@ -233,8 +256,7 @@
         load.start()
 
     barrier = pltpu.get_barrier_semaphore()
-    partners = peers_z + peers_x + peers_g
-    greeted = len(partners)
+    greeted = earlier_first + earlier_second
     for side in SIDES:
         greeted = greeted + goes(*side).astype(jnp.int32)
 
@@ -242,8 +264,11 @@
         def _(side=side):
             pl.semaphore_signal(barrier, inc=1, device_id=beside(*side), device_id_type=MESH)
 
-    for partner in partners:
-        pl.semaphore_signal(barrier, inc=1, device_id=partner, device_id_type=MESH)
+    for _, device, later in peers_first + peers_second:
+
+        @pl.when(later)
+        def _(device=device):
+            pl.semaphore_signal(barrier, inc=1, device_id=device, device_id_type=MESH)
 
     rows = block.reshape(PLANES * ROWS, NZ)
     total_rows = total.reshape(PLANES * ROWS, NZ)
@@ -302,6 +327,14 @@
             pl.when(goes(*side))(copy.start)
 
     start_sides(halo)
+    for number, peers in enumerate((peers_first, peers_second)):
+        for _, device, later in peers:
+
+            @pl.when(jnp.logical_not(later))
+            def _(device=device, number=number):
+                pl.semaphore_signal(
+                    hello.at[number], inc=1, device_id=device, device_id_type=MESH
+                )
 
     for load in loads[1:10]:
         load.wait()
@@ -338,34 +371,50 @@
     y_local, y_middle, y_top = [jnp.sum(value, axis=0, keepdims=True) for value in y_sums]
     row_number = lax.broadcasted_iota(jnp.int32, (8, 128), 0)
     y_rows[...] = jnp.broadcast_to(y_local, (8, 128))
-    sent[0] = jnp.where(row_number == 0, y_middle, y_top)
-
-    def send_sums(stage_number, peers, into, first):
-        copies = []
-        for k, peer in enumerate(peers):
-            copies.append(
-                pltpu.make_async_remote_copy(
-                    src_ref=sent.at[stage_number],
-                    dst_ref=into.at[k],
-                    send_sem=sum_send.at[first + k],
-                    recv_sem=sum_recv.at[first + k],
-                    device_id=peer,
-                    device_id_type=MESH,
-                )
+    sent[0] = jnp.where(row_number == 0, y_middle, y_top)[0:2]
+
+    def sums(peers, source, into, send, recv):
+        return [
+            pltpu.make_async_remote_copy(
+                src_ref=source,
+                dst_ref=into.at[k],
+                send_sem=send.at[k],
+                recv_sem=recv.at[k],
+                device_id=device,
+                device_id_type=MESH,
             )
-        for copy in copies:
-            copy.start()
-        return copies
-
-    def take_sums(copies, stage_number, into):
+            for k, (_, device, _) in enumerate(peers)
+        ]
+
+    first_sums = sums(peers_first, sent.at[0], got_first, first_send, first_recv)
+    second_sums = sums(peers_second, sent.at[1], got_second, second_send, second_recv)
+
+    def take_sums(copies, peers, own, into):
         for copy in copies:
             copy.wait_recv()
-        value = sent[stage_number]
-        for k in range(len(copies)):
-            value = value + into[k]
-        return value
-
-    first_sums = send_sums(0, peers_z, got_z, 0)
+        value = sent[own]
+        others = jnp.zeros_like(value)
+        for k, (same_row, _, _) in enumerate(peers):
+            if same_row:
+                value = value + into[k]
+            else:
+                others = others + into[k]
+        return jnp.where(row_number[0:2] == 0, value, value + others)
+
+    def hear(number, count):
+        @pl.when(count > 0)
+        def _():
+            pl.semaphore_wait(hello.at[number], count)
+
+    hear(0, len(peers_first) - earlier_first)
+    for copy in first_sums:
+        copy.start()
+
+    def forward_sums():
+        sent[1] = take_sums(first_sums, peers_first, 0, got_first)
+        hear(1, len(peers_second) - earlier_second)
+        for copy in second_sums:
+            copy.start()
 
     for load in loads[10:]:
         load.wait()
@@ -471,13 +520,10 @@
                 solved[tile, a, b : b + 4] = value
         return carry
 
-    lax.fori_loop(0, 1, solve, 0)
-    sent[1] = take_sums(first_sums, 0, got_z)
-    second_sums = send_sums(1, peers_x, got_x, 8)
-    lax.fori_loop(1, 2, solve, 0)
+    lax.fori_loop(0, 2, solve, 0)
+    pl.when(jnp.logical_not(middle_z))(forward_sums)
     lax.fori_loop(2, 3, solve, 0)
-    sent[2] = take_sums(second_sums, 1, got_x)
-    third_sums = send_sums(2, peers_g, got_g, 16)
+
     def add_up(a):
         pieces = []
         for tile in range(3):
@@ -516,42 +562,59 @@
     )
     start_sides(rim)
 
-    y_all = take_sums(third_sums, 2, got_g)
-
-    y_local = y_rows[0:1, :]
-    y_middle = sent[2, 0:1, :]
-    y_top = y_all[1:2, :]
-    for part in range(COARSE // 32):
-        here = slice(32 * part, 32 * part + 32)
-        terms = x_local[here, :] * y_local + x_middle[here, :] * y_middle + x_top[here, :] * y_top
-        column = jnp.sum(terms, axis=1, keepdims=True)
-        vertex_col[part : part + 1, :] = jnp.sum(column * eye, axis=0, keepdims=True)
-    vertex_col[20:32, :] = jnp.zeros((12, 32), F32)
-    coarse_high, coarse_low = split(vertex_col[...])
-    spread_out = mm(coarse_high, is_lower) + mm(coarse_low, is_lower)
-    at_vertex = jnp.sum(spread_out * is_upper, axis=0, keepdims=True) * (1.0 / 1728.0)
-    vertex_high, vertex_low = split(is_xy[...] * at_vertex)
-    on_xy = mm_t(vertex_high, hat_zw[...]) + mm_t(vertex_low, hat_zw[...])
-    field_high, field_low = split(on_xy)
-    field = mm(hat_xy[...], field_high) + mm(hat_xy[...], field_low)
     for x in range(NX):
         at = (x + 1) * ROWS
-        out[x] = total_rows[at : at + NY, :] + field[x * ROWS : x * ROWS + NY, :]
-
-    for number, (step_x, step_y) in enumerate(SIDES):
-        x = {1: 0, -1: NX - 1}.get(step_x)
-        y = {1: 0, -1: NY - 1}.get(step_y)
-
-        @pl.when(came(step_x, step_y))
-        def _(number=number, step_x=step_x, step_y=step_y, x=x, y=y):
-            rim[number].wait_recv()
-            if step_y == 0:
-                out[x] = out[x] + x_rim[number]
-            elif step_x == 0:
-                for x in range(NX):
-                    out[x, y : y + 1, :] = out[x, y : y + 1, :] + y_rim[number - 2, x : x + 1, :]
-            else:
-                out[x, y : y + 1, :] = out[x, y : y + 1, :] + c_rim[number - 4]
+        out[x] = total_rows[at : at + NY, :]
+
+    def add_coarse():
+        y_all = take_sums(second_sums, peers_second, 1, got_second)
+        y_local = y_rows[0:1, :]
+        y_middle = y_all[0:1, :]
+        y_top = y_all[1:2, :]
+        for part in range(COARSE // 32):
+            here = slice(32 * part, 32 * part + 32)
+            terms = x_local[here, :] * y_local + x_middle[here, :] * y_middle + x_top[here, :] * y_top
+            column = jnp.sum(terms, axis=1, keepdims=True)
+            vertex_col[part : part + 1, :] = jnp.sum(column * eye, axis=0, keepdims=True)
+        vertex_col[20:32, :] = jnp.zeros((12, 32), F32)
+        coarse_high, coarse_low = split(vertex_col[...])
+        spread_out = mm(coarse_high, is_lower) + mm(coarse_low, is_lower)
+        at_vertex = jnp.sum(spread_out * is_upper, axis=0, keepdims=True) * (1.0 / 1728.0)
+        vertex_high, vertex_low = split(is_xy[...] * at_vertex)
+        on_xy = mm_t(vertex_high, hat_zw[...]) + mm_t(vertex_low, hat_zw[...])
+        field_high, field_low = split(on_xy)
+        field = mm(hat_xy[...], field_high) + mm(hat_xy[...], field_low)
+        for x in range(NX):
+            out[x] = out[x] + field[x * ROWS : x * ROWS + NY, :]
+
+    def add_rims():
+        for number, (step_x, step_y) in enumerate(SIDES):
+            x = {1: 0, -1: NX - 1}.get(step_x)
+            y = {1: 0, -1: NY - 1}.get(step_y)
+
+            @pl.when(came(step_x, step_y))
+            def _(number=number, step_x=step_x, step_y=step_y, x=x, y=y):
+                rim[number].wait_recv()
+                if step_y == 0:
+                    out[x] = out[x] + x_rim[number]
+                elif step_x == 0:
+                    for x in range(NX):
+                        out[x, y : y + 1, :] = (
+                            out[x, y : y + 1, :] + y_rim[number - 2, x : x + 1, :]
+                        )
+                else:
+                    out[x, y : y + 1, :] = out[x, y : y + 1, :] + c_rim[number - 4]
+
+    @pl.when(middle_z)
+    def _():
+        forward_sums()
+        add_rims()
+        add_coarse()
+
+    @pl.when(jnp.logical_not(middle_z))
+    def _():
+        add_coarse()
+        add_rims()
 
     for side, halo_copy, rim_copy in zip(SIDES, halo, rim):
 
@@ -560,7 +623,7 @@
             halo_copy.wait_send()
             rim_copy.wait_send()
 
-    for copy in first_sums + second_sums + third_sums:
+    for copy in first_sums + second_sums:
         copy.wait_send()
 
 
@@ -601,17 +664,19 @@
             pltpu.VMEM((32, 32), F32),
             pltpu.VMEM((32, 32), F32),
             pltpu.VMEM((8, 128), F32),
-            pltpu.VMEM((3, 8, 128), F32),
-            pltpu.VMEM((8, 8, 128), F32),
-            pltpu.VMEM((8, 8, 128), F32),
-            pltpu.VMEM((8, 8, 128), F32),
+            pltpu.VMEM((2, 2, 128), F32),
+            pltpu.VMEM((16, 2, 128), F32),
+            pltpu.VMEM((16, 2, 128), F32),
             pltpu.SemaphoreType.DMA((len(arguments),)),
             pltpu.SemaphoreType.DMA((n_sides,)),
             pltpu.SemaphoreType.DMA((n_sides,)),
             pltpu.SemaphoreType.DMA((n_sides,)),
             pltpu.SemaphoreType.DMA((n_sides,)),
-            pltpu.SemaphoreType.DMA((24,)),
-            pltpu.SemaphoreType.DMA((24,)),
+            pltpu.SemaphoreType.DMA((16,)),
+            pltpu.SemaphoreType.DMA((16,)),
+            pltpu.SemaphoreType.DMA((16,)),
+            pltpu.SemaphoreType.DMA((16,)),
+            pltpu.SemaphoreType.REGULAR((2,)),
         ]
     )
     return pl.pallas_call(

time: 26.3 us -> 25.1 us (0.954); the launches traced: 26.2 us -> 24.7 us
  Pallas kernels: 25.4 us -> 23.9 us
    pallas_call x1, Pallas kernels: 25.4 us -> 23.9 us  [local(): pl.pallas_call(functools.partial(kernel, n_group, n_dev), out_shape=pltpu...]
where the time goes in v5:
time: 25.1 us; the launch traced here: 24.7 us
  Pallas kernels  23.9 us (95%)
  local copies, waits for them, and re-layouts  0.82 us (3%)
    pallas_call x1, Pallas kernels, local(): pl.pallas_call(functools.partial(kernel, n_group, n_dev), out_shape=pltpu...  23.9 us
    unnamed x1, local copies, waits for them, and re-layouts  0.82 us

profile of v5, /device:TPU:1, one launch (start us, length us, event | category | flops | bytes accessed | tf_op | source)
XLA Modules:
  0.0 24.7 jit_solution(6311211074383527991)
XLA Ops:
  0.0 23.9 %shard_map.172 = f32[24,24,144]{2,1,0:T(8,128)S(1)} custom-call(f32[24,24,144]{2,1,0:T(8,128)} %residual.1, f32[192,384]{1,0:T(8,128)} %bitcast.2, f32[24,384]{1,0:T(8,128)} %bitcast.3, s32[8,384]{1,0:T(8,128)} %slot_in.1, f32[640,128]{1,0:T(8,128)} %x_local_in.1, f32[640,128]{1,0:T(8,128)} %x_middle_in.1, f32[640,128]{1,0:T(8,128)} %x_top_in.1, ...), custom_call_target="tpu_custom_call" | custom-call | tf_op jit(solution)/shard_map/pallas_call | solution.py:682
  23.9 0.8 %copy.20 = f32[24,24,144]{2,1,0:T(8,128)} copy(f32[24,24,144]{2,1,0:T(8,128)S(1)} %shard_map.172) | data formatting | bytes 663552

commit v6 on v5

--- a/solution.py
+++ b/solution.py
@@ -60,24 +60,30 @@
     hat_xy = hat_xy.reshape(NX * ROWS, 32)
     hat_zw = np.zeros((NZ, LANES), np.float32)
     is_xy = np.zeros((32, LANES), np.float32)
-    pick_e = np.zeros((ELEMENTS, LANES), np.float32)
-    is_corner = np.zeros((8, LANES), np.float32)
+    others = LANES - ELEMENTS
+    pick_e = np.zeros((ELEMENTS, others), np.float32)
+    is_corner = np.zeros((8, others), np.float32)
+    extra = 0
     for vx in range(5):
         for vy in range(5):
             for vz in range(25):
-                w = (vx * 5 + vy) * 25 + vz
+                i, j, l = min(vx, 3), min(vy, 3), min(vz, 23)
+                corner = 4 * (vx - i) + 2 * (vy - j) + (vz - l)
+                w = (i * BY + j) * BZ + l
+                if corner:
+                    pick_e[w, extra] = 1
+                    is_corner[corner, extra] = 1
+                    w = ELEMENTS + extra
+                    extra += 1
                 hat_zw[:, w] = hat_z[:, vz]
                 is_xy[vx * 5 + vy, w] = 1
-                i, j, l = min(vx, 3), min(vy, 3), min(vz, 23)
-                pick_e[(i * BY + j) * BZ + l, w] = 1
-                is_corner[4 * (vx - i) + 2 * (vy - j) + (vz - l), w] = 1
     return (
         pick_z.astype(bf16),
         pick_z.T.copy().astype(bf16),
         np.concatenate([pick_y, pick_y], axis=0).astype(bf16),
         np.concatenate([pick_y, pick_y], axis=1).astype(bf16),
         order.astype(bf16),
-        hat_xy.astype(bf16),
+        np.concatenate([hat_xy, hat_xy], axis=1).astype(bf16),
         hat_xy.T.copy().astype(bf16),
         hat_zw.astype(bf16),
         pick_e.astype(bf16),
@@ -93,6 +99,12 @@
 
 def mm(a, b):
     return lax.dot_general(a, b, (((1,), (0,)), ((), ())), preferred_element_type=F32)
+
+
+def mm_rows(a, b, product):
+    count = a.shape[0]
+    value = product(jnp.concatenate(split(a), axis=0), b)
+    return value[:count] + value[count:]
 
 
 def mm_t(a, b):
@@ -158,6 +170,7 @@
     values,
     window,
     stage,
+    spare,
     solved,
     total,
     y_halo_pack,
@@ -209,33 +222,33 @@
         return came(-step_x, -step_y)
 
     peers_first, peers_second = [], []
-    for step in range(n_z):
-        for other in range(2):
+    for step in sorted(range(n_z), key=lambda step: -min(step, n_z - step)):
+        for other in (1, 0):
             if step or other:
                 to_z = ahead(at_z, step, n_z)
                 to_core = 1 - core if other else core
                 device = (2 * at_y + to_core, n_z * at_x + to_z)
                 later = 2 * to_z + to_core > 2 * at_z + core
                 peers_first.append((other == 0, device, later))
-    for step in range(n_x):
-        for other in range(n_y):
-            if step or other:
-                to_x, to_y = ahead(at_x, step, n_x), ahead(at_y, other, n_y)
-                device = (2 * to_y + core, n_z * to_x + at_z)
-                later = n_y * to_x + to_y > n_y * at_x + at_y
-                peers_second.append((other == 0, device, later))
+    pairs = [(step, other) for step in range(n_x) for other in range(n_y)]
+    pairs.sort(key=lambda pair: -min(pair[0], n_x - pair[0]) - min(pair[1], n_y - pair[1]))
+    for step, other in pairs:
+        if step or other:
+            to_x, to_y = ahead(at_x, step, n_x), ahead(at_y, other, n_y)
+            device = (2 * to_y + core, n_z * to_x + at_z)
+            later = n_y * to_x + to_y > n_y * at_x + at_y
+            peers_second.append((other == 0, device, later))
     earlier_first = 2 * at_z + core
     earlier_second = n_y * at_x + at_y
-    middle_z = (at_z >= 1) & (at_z <= 3)
 
     pairs = [
+        (slot_in, slot),
+        (pick_e_in, pick_e),
+        (is_corner_in, is_corner),
         (residual, block.at[pl.ds(1, NX), pl.ds(0, NY), :]),
         (hat_xyt_in, hat_xyt),
         (hat_zw_in, hat_zw),
         (is_xy_in, is_xy),
-        (slot_in, slot),
-        (pick_e_in, pick_e),
-        (is_corner_in, is_corner),
         (x_local_in, x_local),
         (x_middle_in, x_middle),
         (x_top_in, x_top),
@@ -308,7 +321,35 @@
             )
         return copies
 
-    loads[0].wait()
+    pl.semaphore_wait(barrier, greeted)
+    def answer(number, peers):
+        for _, device, later in peers:
+
+            @pl.when(jnp.logical_not(later))
+            def _(device=device):
+                pl.semaphore_signal(
+                    hello.at[number], inc=1, device_id=device, device_id_type=MESH
+                )
+
+    def hear(number, count):
+        @pl.when(count > 0)
+        def _():
+            pl.semaphore_wait(hello.at[number], count)
+
+    answer(0, peers_first)
+    for load in loads[0:3]:
+        load.wait()
+    slots = slot[...]
+    parts = jnp.concatenate([(slots >> 5).astype(F32), (slots & 31).astype(F32)], axis=0)
+    picked = mm(parts.astype(BF16), pick_e[...])
+    upper = jnp.sum(picked[0:8] * is_corner[...], axis=0, keepdims=True)
+    lower = jnp.sum(picked[8:16] * is_corner[...], axis=0, keepdims=True)
+    upper = jnp.concatenate([parts[0:1], upper], axis=1)
+    lower = jnp.concatenate([parts[8:9], lower], axis=1)
+    count = lax.broadcasted_iota(jnp.int32, (32, LANES), 0).astype(F32)
+    is_upper = jnp.where(count == upper, 1.0, 0.0)
+    is_lower = jnp.where(count == lower, 1.0, 0.0).astype(BF16)
+    loads[3].wait()
     halo = send_sides(
         rows,
         {1: 24, -1: 1, 0: 0},
@@ -320,40 +361,17 @@
         halo_send,
         halo_recv,
     )
-    pl.semaphore_wait(barrier, greeted)
-
-    def start_sides(copies):
-        for side, copy in zip(SIDES, copies):
-            pl.when(goes(*side))(copy.start)
-
-    start_sides(halo)
-    for number, peers in enumerate((peers_first, peers_second)):
-        for _, device, later in peers:
-
-            @pl.when(jnp.logical_not(later))
-            def _(device=device, number=number):
-                pl.semaphore_signal(
-                    hello.at[number], inc=1, device_id=device, device_id_type=MESH
-                )
-
-    for load in loads[1:10]:
+    for side, copy in reversed(list(zip(SIDES, halo))):
+        pl.when(goes(*side))(copy.start)
+
+    for load in loads[4:10]:
         load.wait()
     own_high, own_low = split(rows[ROWS : ROWS * (NX + 1), :])
     on_xy = mm(hat_xyt[...], own_high) + mm(hat_xyt[...], own_low)
-    on_xy_high, on_xy_low = split(on_xy)
-    on_vertex = mm(on_xy_high, hat_zw[...]) + mm(on_xy_low, hat_zw[...])
+    on_vertex = mm_rows(on_xy, hat_zw[...], mm)
     at_vertex = jnp.sum(on_vertex * is_xy[...], axis=0, keepdims=True) * (1.0 / 1728.0)
 
-    slots = slot[...]
-    parts = jnp.concatenate([(slots >> 5).astype(F32), (slots & 31).astype(F32)], axis=0)
-    picked = mm(parts.astype(BF16), pick_e[...])
-    upper = jnp.sum(picked[0:8] * is_corner[...], axis=0, keepdims=True)
-    lower = jnp.sum(picked[8:16] * is_corner[...], axis=0, keepdims=True)
-    count = lax.broadcasted_iota(jnp.int32, (32, LANES), 0).astype(F32)
-    is_upper = jnp.where(count == upper, 1.0, 0.0)
-    is_lower = jnp.where(count == lower, 1.0, 0.0).astype(BF16)
-    by_high, by_low = split(is_upper * at_vertex)
-    small[...] = mm_t(by_high, is_lower) + mm_t(by_low, is_lower)
+    small[...] = mm_rows(is_upper * at_vertex, is_lower, mm_t)
 
     eye = jnp.where(
         lax.broadcasted_iota(jnp.int32, (32, 32), 0) == lax.broadcasted_iota(jnp.int32, (32, 32), 1),
@@ -401,14 +419,10 @@
                 others = others + into[k]
         return jnp.where(row_number[0:2] == 0, value, value + others)
 
-    def hear(number, count):
-        @pl.when(count > 0)
-        def _():
-            pl.semaphore_wait(hello.at[number], count)
-
     hear(0, len(peers_first) - earlier_first)
     for copy in first_sums:
         copy.start()
+    answer(1, peers_second)
 
     def forward_sums():
         sent[1] = take_sums(first_sums, peers_first, 0, got_first)
@@ -484,21 +498,27 @@
                     term = bcast(vectors, tile, 64 + b * 8 + q) * fields[b]
                     value = term if value is None else value + term
                 turned.append(value)
+            for q in range(8):
+                spare[q] = turned[q]
             along = [vectors[tile, 128 + 8 * c : 136 + 8 * c, :] for c in range(8)]
             scale = bcast(values, tile, p) + values[tile, 16:24, :]
             divided = []
             for q in range(8):
                 value = None
                 for c in range(8):
-                    term = along[c] * turned[q][c : c + 1, :]
+                    term = along[c] * spare[q, pl.ds(c, 8, stride=0), :]
                     value = term if value is None else value + term
-                divided.append(value / (scale + bcast(values, tile, 8 + q)))
+                below = scale + bcast(values, tile, 8 + q)
+                inverse = pl.reciprocal(below, approx=True)
+                divided.append(value * (inverse * (2.0 - below * inverse)))
+            for q in range(8):
+                spare[8 + q] = divided[q]
             across = [vectors[tile, pl.ds(128 + s, 8, stride=8), :] for s in range(8)]
             back = []
             for q in range(8):
                 value = None
                 for s in range(8):
-                    term = across[s] * divided[q][s : s + 1, :]
+                    term = across[s] * spare[8 + q, pl.ds(s, 8, stride=0), :]
                     value = term if value is None else value + term
                 back.append(value)
             for b in range(8):
@@ -509,7 +529,7 @@
                 stage[p, b] = value
             return carry
 
-        lax.fori_loop(0, 8, middle, 0)
+        lax.fori_loop(0, 8, middle, 0, unroll=2)
         for b in (0, 4):
             fields = [stage[p, b : b + 4] for p in range(8)]
             for a in range(8):
@@ -520,9 +540,9 @@
                 solved[tile, a, b : b + 4] = value
         return carry
 
-    lax.fori_loop(0, 2, solve, 0)
-    pl.when(jnp.logical_not(middle_z))(forward_sums)
-    lax.fori_loop(2, 3, solve, 0)
+    lax.fori_loop(0, 1, solve, 0)
+    forward_sums()
+    lax.fori_loop(1, 3, solve, 0)
 
     def add_up(a):
         pieces = []
@@ -560,7 +580,8 @@
         rim_send,
         rim_recv,
     )
-    start_sides(rim)
+    for side, copy in reversed(list(zip(SIDES, rim))):
+        pl.when(goes(*side))(copy.start)
 
     for x in range(NX):
         at = (x + 1) * ROWS
@@ -577,13 +598,10 @@
             column = jnp.sum(terms, axis=1, keepdims=True)
             vertex_col[part : part + 1, :] = jnp.sum(column * eye, axis=0, keepdims=True)
         vertex_col[20:32, :] = jnp.zeros((12, 32), F32)
-        coarse_high, coarse_low = split(vertex_col[...])
-        spread_out = mm(coarse_high, is_lower) + mm(coarse_low, is_lower)
+        spread_out = mm_rows(vertex_col[...], is_lower, mm)
         at_vertex = jnp.sum(spread_out * is_upper, axis=0, keepdims=True) * (1.0 / 1728.0)
-        vertex_high, vertex_low = split(is_xy[...] * at_vertex)
-        on_xy = mm_t(vertex_high, hat_zw[...]) + mm_t(vertex_low, hat_zw[...])
-        field_high, field_low = split(on_xy)
-        field = mm(hat_xy[...], field_high) + mm(hat_xy[...], field_low)
+        on_xy = mm_rows(is_xy[...] * at_vertex, hat_zw[...], mm_t)
+        field = mm(hat_xy[...], jnp.concatenate(split(on_xy), axis=0))
         for x in range(NX):
             out[x] = out[x] + field[x * ROWS : x * ROWS + NY, :]
 
@@ -605,16 +623,8 @@
                 else:
                     out[x, y : y + 1, :] = out[x, y : y + 1, :] + c_rim[number - 4]
 
-    @pl.when(middle_z)
-    def _():
-        forward_sums()
-        add_rims()
-        add_coarse()
-
-    @pl.when(jnp.logical_not(middle_z))
-    def _():
-        add_coarse()
-        add_rims()
+    add_coarse()
+    add_rims()
 
     for side, halo_copy, rim_copy in zip(SIDES, halo, rim):
 
@@ -649,6 +659,7 @@
             pltpu.VMEM((3, 24, 128), F32),
             pltpu.VMEM((3, 8, 8, 8, 128), F32),
             pltpu.VMEM((8, 8, 8, 128), F32),
+            pltpu.VMEM((16, 8, 128), F32),
             pltpu.VMEM((3, 8, 8, 8, 128), F32),
             pltpu.VMEM((PLANES, ROWS, NZ), F32),
             pltpu.VMEM((2, 24, NZ), F32),

time: 25.1 us -> 24.3 us (0.968)
  Pallas kernels: 23.9 us -> 23 us
    pallas_call x1, Pallas kernels: 23.9 us -> 23 us  [local(): pl.pallas_call(functools.partial(kernel, n_group, n_dev), out_shape=pltpu...]
where the time goes in v6:
time: 24.3 us; the launch traced here: 23.8 us
  Pallas kernels  23 us (95%)
  local copies, waits for them, and re-layouts  0.82 us (3%)
    pallas_call x1, Pallas kernels, local(): pl.pallas_call(functools.partial(kernel, n_group, n_dev), out_shape=pltpu...  23 us
    unnamed x1, local copies, waits for them, and re-layouts  0.82 us

profile of v6, /device:TPU:1, one launch (start us, length us, event | category | flops | bytes accessed | tf_op | source)
XLA Modules:
  0.0 23.8 jit_solution(14633625524805352769)
XLA Ops:
  0.0 23.0 %shard_map.172 = f32[24,24,144]{2,1,0:T(8,128)S(1)} custom-call(f32[24,24,144]{2,1,0:T(8,128)} %residual.1, f32[192,384]{1,0:T(8,128)} %bitcast.2, f32[24,384]{1,0:T(8,128)} %bitcast.3, s32[8,384]{1,0:T(8,128)} %slot_in.1, f32[640,128]{1,0:T(8,128)} %x_local_in.1, f32[640,128]{1,0:T(8,128)} %x_middle_in.1, f32[640,128]{1,0:T(8,128)} %x_top_in.1, ...), custom_call_target="tpu_custom_call" | custom-call | tf_op jit(solution)/shard_map/pallas_call | solution.py:693
  23.0 0.8 %copy.20 = f32[24,24,144]{2,1,0:T(8,128)} copy(f32[24,24,144]{2,1,0:T(8,128)S(1)} %shard_map.172) | data formatting | bytes 663552

commit v7 on v6

--- a/solution.py
+++ b/solution.py
@@ -40,6 +40,11 @@
         for b in range(8):
             for j in range(4):
                 pick_y[i * 32 + row_of(6 * j + b), i * 32 + b * 4 + j] = 1
+    pick_side = np.zeros((2, 2, NX, 6, 4, 8, 4), np.float32)
+    for x in range(NX):
+        for side, j in enumerate((0, 3)):
+            pick_side[:, side, x, x % 6, x // 6, :, j] = 1
+    pick_side = pick_side.reshape(96, 768)
     order = np.zeros((ELEMENTS, ELEMENTS), np.float32)
     for i in range(BX):
         for j in range(BY):
@@ -83,6 +88,7 @@
         np.concatenate([pick_y, pick_y], axis=0).astype(bf16),
         np.concatenate([pick_y, pick_y], axis=1).astype(bf16),
         order.astype(bf16),
+        pick_side.astype(bf16),
         np.concatenate([hat_xy, hat_xy], axis=1).astype(bf16),
         hat_xy.T.copy().astype(bf16),
         hat_zw.astype(bf16),
@@ -141,6 +147,7 @@
     pick_y_in,
     pick_yt_in,
     order_in,
+    pick_side_in,
     hat_xy_in,
     hat_xyt_in,
     hat_zw_in,
@@ -160,6 +167,7 @@
     pick_y,
     pick_yt,
     order,
+    pick_side,
     hat_xy,
     hat_xyt,
     hat_zw,
@@ -255,6 +263,7 @@
         (vectors_in, vectors_raw),
         (values_in, values_raw),
         (order_in, order),
+        (pick_side_in, pick_side),
         (pick_z_in, pick_z),
         (pick_y_in, pick_y),
         (pick_yt_in, pick_yt),
@@ -337,18 +346,6 @@
             pl.semaphore_wait(hello.at[number], count)
 
     answer(0, peers_first)
-    for load in loads[0:3]:
-        load.wait()
-    slots = slot[...]
-    parts = jnp.concatenate([(slots >> 5).astype(F32), (slots & 31).astype(F32)], axis=0)
-    picked = mm(parts.astype(BF16), pick_e[...])
-    upper = jnp.sum(picked[0:8] * is_corner[...], axis=0, keepdims=True)
-    lower = jnp.sum(picked[8:16] * is_corner[...], axis=0, keepdims=True)
-    upper = jnp.concatenate([parts[0:1], upper], axis=1)
-    lower = jnp.concatenate([parts[8:9], lower], axis=1)
-    count = lax.broadcasted_iota(jnp.int32, (32, LANES), 0).astype(F32)
-    is_upper = jnp.where(count == upper, 1.0, 0.0)
-    is_lower = jnp.where(count == lower, 1.0, 0.0).astype(BF16)
     loads[3].wait()
     halo = send_sides(
         rows,
@@ -364,6 +361,18 @@
     for side, copy in reversed(list(zip(SIDES, halo))):
         pl.when(goes(*side))(copy.start)
 
+    for load in loads[0:3]:
+        load.wait()
+    slots = slot[...]
+    parts = jnp.concatenate([(slots >> 5).astype(F32), (slots & 31).astype(F32)], axis=0)
+    picked = mm(parts.astype(BF16), pick_e[...])
+    upper = jnp.sum(picked[0:8] * is_corner[...], axis=0, keepdims=True)
+    lower = jnp.sum(picked[8:16] * is_corner[...], axis=0, keepdims=True)
+    upper = jnp.concatenate([parts[0:1], upper], axis=1)
+    lower = jnp.concatenate([parts[8:9], lower], axis=1)
+    count = lax.broadcasted_iota(jnp.int32, (32, LANES), 0).astype(F32)
+    is_upper = jnp.where(count == upper, 1.0, 0.0)
+    is_lower = jnp.where(count == lower, 1.0, 0.0).astype(BF16)
     for load in loads[4:10]:
         load.wait()
     own_high, own_low = split(rows[ROWS : ROWS * (NX + 1), :])
@@ -419,9 +428,8 @@
                 others = others + into[k]
         return jnp.where(row_number[0:2] == 0, value, value + others)
 
-    hear(0, len(peers_first) - earlier_first)
-    for copy in first_sums:
-        copy.start()
+    for (_, _, later), copy in zip(peers_first, first_sums):
+        pl.when(jnp.logical_not(later))(copy.start)
     answer(1, peers_second)
 
     def forward_sums():
@@ -438,22 +446,6 @@
     for tile in range(3):
         vectors[tile] = ordered[0:192, 128 * tile : 128 * tile + 128]
         values[tile] = ordered[192:216, 128 * tile : 128 * tile + 128]
-
-    for number, (step_x, step_y) in enumerate(SIDES):
-        plane = {1: 0, -1: PLANES - 1}.get(step_x)
-        row = {1: 24, -1: 25}.get(step_y)
-
-        @pl.when(came(step_x, step_y))
-        def _(number=number, step_x=step_x, step_y=step_y, plane=plane, row=row):
-            halo[number].wait_recv()
-            if step_y == 0:
-                rows[plane * ROWS : plane * ROWS + 24, :] = x_halo[number]
-            elif step_x == 0:
-                for x in range(NX):
-                    at = (x + 1) * ROWS + row
-                    rows[at : at + 1, :] = y_halo[number - 2, x : x + 1, :]
-            else:
-                rows[plane * ROWS + row : plane * ROWS + row + 1, :] = c_halo[number - 4]
 
     lane = lax.broadcasted_iota(jnp.int32, (8, 128), 1)
     masks = [(lane >> (2 + bit)) & 1 == 1 for bit in range(3)]
@@ -474,7 +466,46 @@
                 window[tile, a, b] = pieces[b]
         return carry
 
-    lax.fori_loop(0, 8, make_windows, 0, unroll=8)
+    hear(0, len(peers_first) - earlier_first)
+    for (_, _, later), copy in zip(peers_first, first_sums):
+        pl.when(later)(copy.start)
+
+    lax.fori_loop(1, 7, make_windows, 0, unroll=6)
+
+    for number, (step_x, step_y) in enumerate(SIDES):
+        plane = {1: 0, -1: PLANES - 1}.get(step_x)
+        row = {1: 24, -1: 25}.get(step_y)
+
+        @pl.when(came(step_x, step_y))
+        def _(number=number, step_x=step_x, step_y=step_y, plane=plane, row=row):
+            halo[number].wait_recv()
+            if step_y == 0:
+                rows[plane * ROWS : plane * ROWS + 24, :] = x_halo[number]
+            elif step_x == 0:
+                for x in range(NX):
+                    at = (x + 1) * ROWS + row
+                    rows[at : at + 1, :] = y_halo[number - 2, x : x + 1, :]
+            else:
+                rows[plane * ROWS + row : plane * ROWS + row + 1, :] = c_halo[number - 4]
+
+    sides = [
+        jnp.where(came(0, step), y_halo[number], 0.0) for number, step in enumerate((1, -1))
+    ]
+    both = jnp.concatenate(split(jnp.concatenate(sides, axis=0)), axis=0)
+    beyond = mm(mm_t(pick_z[...], both).astype(BF16), pick_side[...])
+    at_l = lane >> 2 & 7
+    at_j = lane & 3
+    for a in range(1, 7):
+        column = slice(128 * (a - 1), 128 * a)
+        for tile in range(3):
+            value = jnp.zeros((8, 128), F32)
+            for l in range(8):
+                first = tile * 64 + 8 * l
+                value = jnp.where(at_l == l, beyond[first : first + 8, column], value)
+            window[tile, a, 0] = window[tile, a, 0] + jnp.where(at_j == 0, value, 0.0)
+            window[tile, a, 7] = window[tile, a, 7] + jnp.where(at_j == 3, value, 0.0)
+    make_windows(0, 0)
+    make_windows(7, 0)
 
     def bcast(ref, tile, row):
         return ref[tile, pl.ds(row, 8, stride=0), :]
@@ -583,10 +614,6 @@
     for side, copy in reversed(list(zip(SIDES, rim))):
         pl.when(goes(*side))(copy.start)
 
-    for x in range(NX):
-        at = (x + 1) * ROWS
-        out[x] = total_rows[at : at + NY, :]
-
     def add_coarse():
         y_all = take_sums(second_sums, peers_second, 1, got_second)
         y_local = y_rows[0:1, :]
@@ -603,7 +630,8 @@
         on_xy = mm_rows(is_xy[...] * at_vertex, hat_zw[...], mm_t)
         field = mm(hat_xy[...], jnp.concatenate(split(on_xy), axis=0))
         for x in range(NX):
-            out[x] = out[x] + field[x * ROWS : x * ROWS + NY, :]
+            at = (x + 1) * ROWS
+            out[x] = total_rows[at : at + NY, :] + field[x * ROWS : x * ROWS + NY, :]
 
     def add_rims():
         for number, (step_x, step_y) in enumerate(SIDES):

time: 24.3 us -> 24.2 us (level)
  the two profiles are of different devices: /device:TPU:1 before, /device:TPU:6 now
where the time goes in v7:
time: 24.2 us; the launch traced here: 24.1 us
  Pallas kernels  23.3 us (96%)
  local copies, waits for them, and re-layouts  0.82 us (3%)
    pallas_call x1, Pallas kernels, local(): pl.pallas_call(functools.partial(kernel, n_group, n_dev), out_shape=pltpu...  23.3 us
    unnamed x1, local copies, waits for them, and re-layouts  0.82 us

profile of v7, /device:TPU:6, one launch (start us, length us, event | category | flops | bytes accessed | tf_op | source)
XLA Modules:
  0.0 24.1 jit_solution(15239293560534388487)
XLA Ops:
  0.0 23.3 %shard_map.181 = f32[24,24,144]{2,1,0:T(8,128)S(1)} custom-call(f32[24,24,144]{2,1,0:T(8,128)} %residual.1, f32[192,384]{1,0:T(8,128)} %bitcast.2, f32[24,384]{1,0:T(8,128)} %bitcast.3, s32[8,384]{1,0:T(8,128)} %slot_in.1, f32[640,128]{1,0:T(8,128)} %x_local_in.1, f32[640,128]{1,0:T(8,128)} %x_middle_in.1, f32[640,128]{1,0:T(8,128)} %x_top_in.1, ...), custom_call_target="tpu_custom_call" | custom-call | tf_op jit(solution)/shard_map/pallas_call | solution.py:721
  23.3 0.8 %copy.21 = f32[24,24,144]{2,1,0:T(8,128)} copy(f32[24,24,144]{2,1,0:T(8,128)S(1)} %shard_map.181) | data formatting | bytes 663552

commit v8 on v7

--- a/solution.py
+++ b/solution.py
@@ -530,7 +530,7 @@
                     value = term if value is None else value + term
                 turned.append(value)
             for q in range(8):
-                spare[q] = turned[q]
+                spare[q, 0:8, :] = turned[q]
             along = [vectors[tile, 128 + 8 * c : 136 + 8 * c, :] for c in range(8)]
             scale = bcast(values, tile, p) + values[tile, 16:24, :]
             divided = []
@@ -543,7 +543,7 @@
                 inverse = pl.reciprocal(below, approx=True)
                 divided.append(value * (inverse * (2.0 - below * inverse)))
             for q in range(8):
-                spare[8 + q] = divided[q]
+                spare[8 + q, 0:8, :] = divided[q]
             across = [vectors[tile, pl.ds(128 + s, 8, stride=8), :] for s in range(8)]
             back = []
             for q in range(8):
@@ -687,7 +687,7 @@
             pltpu.VMEM((3, 24, 128), F32),
             pltpu.VMEM((3, 8, 8, 8, 128), F32),
             pltpu.VMEM((8, 8, 8, 128), F32),
-            pltpu.VMEM((16, 8, 128), F32),
+            pltpu.VMEM((16, 16, 128), F32),
             pltpu.VMEM((3, 8, 8, 8, 128), F32),
             pltpu.VMEM((PLANES, ROWS, NZ), F32),
             pltpu.VMEM((2, 24, NZ), F32),

time: 24.2 us -> 24.2 us (level)
  no operation moved by 1% of the time
where the time goes in v8:
time: 24.2 us; the launch traced here: 24.1 us
  Pallas kernels  23.2 us (96%)
  local copies, waits for them, and re-layouts  0.82 us (3%)
    pallas_call x1, Pallas kernels, local(): pl.pallas_call(functools.partial(kernel, n_group, n_dev), out_shape=pltpu...  23.2 us
    unnamed x1, local copies, waits for them, and re-layouts  0.82 us

profile of v8, /device:TPU:6, one launch (start us, length us, event | category | flops | bytes accessed | tf_op | source)
XLA Modules:
  0.0 24.1 jit_solution(12024672189486580089)
XLA Ops:
  0.0 23.2 %shard_map.181 = f32[24,24,144]{2,1,0:T(8,128)S(1)} custom-call(f32[24,24,144]{2,1,0:T(8,128)} %residual.1, f32[192,384]{1,0:T(8,128)} %bitcast.2, f32[24,384]{1,0:T(8,128)} %bitcast.3, s32[8,384]{1,0:T(8,128)} %slot_in.1, f32[640,128]{1,0:T(8,128)} %x_local_in.1, f32[640,128]{1,0:T(8,128)} %x_middle_in.1, f32[640,128]{1,0:T(8,128)} %x_top_in.1, ...), custom_call_target="tpu_custom_call" | custom-call | tf_op jit(solution)/shard_map/pallas_call | solution.py:721
  23.3 0.8 %copy.21 = f32[24,24,144]{2,1,0:T(8,128)} copy(f32[24,24,144]{2,1,0:T(8,128)S(1)} %shard_map.181) | data formatting | bytes 663552
